TPU v7x, 512 devices: a whole 4x8x8 slice. The times are simulated.
512 devices in a mesh: depth: 32 (over y, z_hi), xline: 16 (over x, z_lo, core).
Axes of the slice: x: 4, y: 8, z: 8 (z_hi: 4, z_lo: 2; z = z_hi * 2 + z_lo), core: 2. Of those that a mesh axis runs over, the one named last changes fastest.
Arguments:
- surface_fields: float32 [2, 2, 2, 256, 128], P(None, None, None, 'xline'), may hold values from -6 to 6
- stencil_table: float32 [13, 2, 2, 128], replicated
- velocity_bins: int32 [32, 2, 256, 128], P('depth', None, 'xline'), may hold values from 0 to 127
- offset_list: int32 [16, 2], replicated, may hold values from -8 to 8, as said below
Outputs:
- image_tiles: float32 [32, 16, 256, 128], P('depth', None, 'xline')
Inputs may be any that keep to these rules, and one draw needn't show every extreme that they name: `offset_list`: column 0 lies within -8 to 8 and column 1 within -8 to 8; both ends of both ranges occur in every draw.
All inputs are finite; a program needn't handle non-finite values.
Results may differ from a plain program's by a relative error of at most 0.0003.
Values sent between devices are 32-bit elements; how exact they have to be, the bound alone decides.
A program may use at most 64 MiB of HBM per device.

v0:
```python
import jax
import jax.numpy as jnp
from jax import lax
from jax.sharding import PartitionSpec as P

OFF_Y = 8
OFF_X = 8


tap_rows = (0, -4, -3, -2, -1, 1, 2, 3, 4, 0, 0, 0, 0)
tap_cols = (0, 0, 0, 0, 0, 0, 0, 0, 0, -2, -1, 1, 2)
reach_rows = 4
reach_cols = 2


def with_halo(array, sides, width):
    for axis, dim in sides:
        count, length = (lax.axis_size(axis), array.shape[dim])
        up = [(i, (i + 1) % count) for i in range(count - 1)]
        down = [(j, i) for i, j in up]
        last = lax.slice_in_dim(array, length - width, length, axis=dim)
        leading = lax.slice_in_dim(array, 0, width, axis=dim)
        before = lax.ppermute(last, axis, up)
        after = lax.ppermute(leading, axis, down)
        array = jnp.concatenate([before, array, after], axis=dim)
    return array


def shifted_2(block, axis, distance):
    devices = range(lax.axis_size(axis))
    route = [(i - distance, i) for i in devices if i - distance in devices]
    return lax.ppermute(block, axis, route)


def extrapolate(fields, coefficients):
    row_count = fields.shape[3] - 2 * reach_rows
    inline_width = fields.shape[4]
    padded = jnp.pad(fields, ((0, 0), (0, 0), (0, 0), (0, 0), (reach_cols, reach_cols)))
    conj_sign = jnp.array([1.0, -1.0], dtype=jnp.float32).reshape(2, 1, 1, 1)
    real_part = None
    imag_part = None
    for tap_index in range(len(tap_rows)):
        first_row = reach_rows + tap_rows[tap_index]
        first_col = reach_cols + tap_cols[tap_index]
        shifted = padded[
            :, :, :, first_row : first_row + row_count, first_col : first_col + inline_width
        ]
        coef_real = coefficients[tap_index, 0]
        coef_imag = coefficients[tap_index, 1] * conj_sign
        term_real = coef_real * shifted[:, 0] - coef_imag * shifted[:, 1]
        term_imag = coef_real * shifted[:, 1] + coef_imag * shifted[:, 0]
        if tap_index == 0:
            real_part = term_real
            imag_part = term_imag
        else:
            real_part = real_part + term_real
            imag_part = imag_part + term_imag
    return jnp.stack([real_part, imag_part], axis=1)


def correlate(source, receiver, offset_list):
    padded = jnp.pad(receiver, ((0, 0), (0, 0), (0, 0), (OFF_X, OFF_X)))
    slice_shape = (2, source.shape[1], source.shape[2], source.shape[3])

    def one_offset(offset_couple):
        starts = (jnp.int32(0), jnp.int32(0), OFF_Y + offset_couple[0], OFF_X + offset_couple[1])
        shifted = lax.dynamic_slice(padded, starts, slice_shape)
        return jnp.sum(source[0] * shifted[0] + source[1] * shifted[1], axis=0)

    return jax.vmap(one_offset)(offset_list)


def within_mesh(first_row, span_rows, grid_rows):
    row_ids = first_row + jnp.arange(span_rows, dtype=jnp.int32)
    return ((row_ids >= 0) & (row_ids < grid_rows)).astype(jnp.float32)[:, None]


def shards(surface_fields, stencil_table, velocity_bins, offset_list):
    depth_count = lax.axis_size("depth")
    depth_index = lax.axis_index("depth")
    crossline_index = lax.axis_index("xline")
    row_count = surface_fields.shape[3]
    inline_width = surface_fields.shape[4]
    freq_count = surface_fields.shape[2]
    grid_rows = row_count * lax.axis_size("xline")
    base_row = crossline_index * row_count
    group_size = 1
    group_count = freq_count // group_size
    section_count = depth_count + group_count - 1
    slab_velocity = velocity_bins[0]
    margin = reach_rows + OFF_Y
    extended = with_halo(slab_velocity, (("xline", 1),), reach_rows + OFF_Y)
    ext_rows = row_count + 2 * margin
    vel_count = stencil_table.shape[3]
    flat_table = stencil_table.reshape(-1, vel_count)
    bin_ids = jnp.arange(vel_count, dtype=jnp.int32)[:, None]
    level_tables = []
    for level_index in range(velocity_bins.shape[1]):
        onehot = (bin_ids == extended[level_index].reshape(1, -1)).astype(jnp.float32)
        product = jnp.dot(
            flat_table, onehot, precision=lax.Precision.HIGHEST, preferred_element_type=jnp.float32
        )
        level_tables.append(
            product.reshape(stencil_table.shape[0], 2, freq_count, ext_rows, inline_width)
        )
    coefficients = jnp.stack(level_tables)

    def advance(section_index, state_pair):
        outgoing, image_tile = state_pair
        group_index = section_index - depth_index
        active = (group_index >= 0) & (group_index < group_count)
        clipped = jnp.clip(group_index, 0, group_count - 1)
        incoming = shifted_2(outgoing, "depth", 1)
        fresh = lax.dynamic_slice_in_dim(surface_fields, clipped * group_size, group_size, 2)
        fields = jnp.where(depth_index == 0, fresh, incoming)
        level_coefs = lax.dynamic_slice_in_dim(coefficients, clipped * group_size, group_size, 3)
        padded = with_halo(fields, (("xline", 3),), 2 * reach_rows + OFF_Y)
        upper = extrapolate(padded, level_coefs[0]) * within_mesh(
            base_row - margin, ext_rows, grid_rows
        )
        lower_rows = row_count + 2 * OFF_Y
        lower = extrapolate(upper, level_coefs[1][:, :, :, reach_rows : reach_rows + lower_rows])
        lower = lower * within_mesh(base_row - OFF_Y, lower_rows, grid_rows)
        fields = lower[:, :, :, OFF_Y : OFF_Y + row_count]
        receiver = lower[1]
        image_tile = image_tile + jnp.where(
            active, correlate(fields[0], receiver, offset_list), 0.0
        )
        return (fields, image_tile)

    start_fields = jnp.zeros((2, 2, group_size, row_count, inline_width), jnp.float32)
    start_image = jnp.zeros((offset_list.shape[0], row_count, inline_width), jnp.float32)
    final_fields, image_tile = lax.fori_loop(0, section_count, advance, (start_fields, start_image))
    return image_tile[None]


def solution(mesh):
    return jax.shard_map(
        shards,
        mesh=mesh,
        in_specs=(P(None, None, None, "xline", None), P(), P("depth", None, "xline", None), P()),
        out_specs=P("depth", None, "xline", None),
        check_vma=False,
    )
```

profile of v0, /device:TPU:34, one launch (start us, length us, event | category | flops | bytes accessed | tf_op | source)
XLA Modules:
  0.0 1712.7 jit_solution(15178469092622921471)
XLA Ops:
  12.7 1699.3 %while.27 = (s32[]{:T(128)}, f32[2,2,1,16,128]{4,3,1,2,0:T(8,128)S(1)}, f32[16,16,128]{2,1,0:T(8,128)S(1)}, s32[]{:T(128)}, f32[2,13,2,2,40,128]{5,4,3,2,1,0:T(8...) while((s32[]{:T(128)}, ...), condition=%wide.region_1.2_spmd.clone.clone.clone, body=%wide.region_0.1_spmd.sunk.clone.clone.clone.sunk | while | flops 2687603 | bytes 13050807 | solution.py:133
  38.5 30.0 %while.28 = (s32[]{:T(128)}, f32[2,1,32,144]{3,2,1,0:T(8,128)S(1)}, s32[16,4]{0,1:T(4,128)S(1)}, f32[16,2,1,16,128]{4,3,0,2,1:T(8,128)S(1)}, s32[]{:T(128)}) while((s32[]{:T(128)}, f32[2,1,32,144]{3,2,1,0:T(8,128)S(1)}, s32[16,4]{0,1:T(4,128)S(1)}, f32[16,2,1,16,128]{4,3,0,2,1:T(8,128)S(1)}, s32[]{:T(128)}) %tuple.138), condition=%wide.while_cond, body=%wide.while_body.sunk | while | flops 2 | bytes 32893 | solution.py:67
  89.8 30.0 %while.28 = (s32[]{:T(128)}, f32[2,1,32,144]{3,2,1,0:T(8,128)S(1)}, s32[16,4]{0,1:T(4,128)S(1)}, f32[16,2,1,16,128]{4,3,0,2,1:T(8,128)S(1)}, s32[]{:T(128)}) while((s32[]{:T(128)}, f32[2,1,32,144]{3,2,1,0:T(8,128)S(1)}, s32[16,4]{0,1:T(4,128)S(1)}, f32[16,2,1,16,128]{4,3,0,2,1:T(8,128)S(1)}, s32[]{:T(128)}) %tuple.138), condition=%wide.while_cond, body=%wide.while_body.sunk | while | flops 2 | bytes 32893 | solution.py:67
  123.5 6.4 collective-permute-done
  141.2 30.0 %while.28 = (s32[]{:T(128)}, f32[2,1,32,144]{3,2,1,0:T(8,128)S(1)}, s32[16,4]{0,1:T(4,128)S(1)}, f32[16,2,1,16,128]{4,3,0,2,1:T(8,128)S(1)}, s32[]{:T(128)}) while((s32[]{:T(128)}, f32[2,1,32,144]{3,2,1,0:T(8,128)S(1)}, s32[16,4]{0,1:T(4,128)S(1)}, f32[16,2,1,16,128]{4,3,0,2,1:T(8,128)S(1)}, s32[]{:T(128)}) %tuple.138), condition=%wide.while_cond, body=%wide.while_body.sunk | while | flops 2 | bytes 32893 | solution.py:67
  192.5 30.0 %while.28 = (s32[]{:T(128)}, f32[2,1,32,144]{3,2,1,0:T(8,128)S(1)}, s32[16,4]{0,1:T(4,128)S(1)}, f32[16,2,1,16,128]{4,3,0,2,1:T(8,128)S(1)}, s32[]{:T(128)}) while((s32[]{:T(128)}, f32[2,1,32,144]{3,2,1,0:T(8,128)S(1)}, s32[16,4]{0,1:T(4,128)S(1)}, f32[16,2,1,16,128]{4,3,0,2,1:T(8,128)S(1)}, s32[]{:T(128)}) %tuple.138), condition=%wide.while_cond, body=%wide.while_body.sunk | while | flops 2 | bytes 32893 | solution.py:67
  226.2 6.4 collective-permute-done
  243.9 30.0 %while.28 = (s32[]{:T(128)}, f32[2,1,32,144]{3,2,1,0:T(8,128)S(1)}, s32[16,4]{0,1:T(4,128)S(1)}, f32[16,2,1,16,128]{4,3,0,2,1:T(8,128)S(1)}, s32[]{:T(128)}) while((s32[]{:T(128)}, f32[2,1,32,144]{3,2,1,0:T(8,128)S(1)}, s32[16,4]{0,1:T(4,128)S(1)}, f32[16,2,1,16,128]{4,3,0,2,1:T(8,128)S(1)}, s32[]{:T(128)}) %tuple.138), condition=%wide.while_cond, body=%wide.while_body.sunk | while | flops 2 | bytes 32893 | solution.py:67
  277.6 6.4 collective-permute-done
  295.3 30.0 %while.28 = (s32[]{:T(128)}, f32[2,1,32,144]{3,2,1,0:T(8,128)S(1)}, s32[16,4]{0,1:T(4,128)S(1)}, f32[16,2,1,16,128]{4,3,0,2,1:T(8,128)S(1)}, s32[]{:T(128)}) while((s32[]{:T(128)}, f32[2,1,32,144]{3,2,1,0:T(8,128)S(1)}, s32[16,4]{0,1:T(4,128)S(1)}, f32[16,2,1,16,128]{4,3,0,2,1:T(8,128)S(1)}, s32[]{:T(128)}) %tuple.138), condition=%wide.while_cond, body=%wide.while_body.sunk | while | flops 2 | bytes 32893 | solution.py:67
  329.0 6.4 collective-permute-done
  346.7 30.0 %while.28 = (s32[]{:T(128)}, f32[2,1,32,144]{3,2,1,0:T(8,128)S(1)}, s32[16,4]{0,1:T(4,128)S(1)}, f32[16,2,1,16,128]{4,3,0,2,1:T(8,128)S(1)}, s32[]{:T(128)}) while((s32[]{:T(128)}, f32[2,1,32,144]{3,2,1,0:T(8,128)S(1)}, s32[16,4]{0,1:T(4,128)S(1)}, f32[16,2,1,16,128]{4,3,0,2,1:T(8,128)S(1)}, s32[]{:T(128)}) %tuple.138), condition=%wide.while_cond, body=%wide.while_body.sunk | while | flops 2 | bytes 32893 | solution.py:67
  380.4 6.4 collective-permute-done
  398.0 30.0 %while.28 = (s32[]{:T(128)}, f32[2,1,32,144]{3,2,1,0:T(8,128)S(1)}, s32[16,4]{0,1:T(4,128)S(1)}, f32[16,2,1,16,128]{4,3,0,2,1:T(8,128)S(1)}, s32[]{:T(128)}) while((s32[]{:T(128)}, f32[2,1,32,144]{3,2,1,0:T(8,128)S(1)}, s32[16,4]{0,1:T(4,128)S(1)}, f32[16,2,1,16,128]{4,3,0,2,1:T(8,128)S(1)}, s32[]{:T(128)}) %tuple.138), condition=%wide.while_cond, body=%wide.while_body.sunk | while | flops 2 | bytes 32893 | solution.py:67
  431.7 6.4 collective-permute-done
  449.4 30.0 %while.28 = (s32[]{:T(128)}, f32[2,1,32,144]{3,2,1,0:T(8,128)S(1)}, s32[16,4]{0,1:T(4,128)S(1)}, f32[16,2,1,16,128]{4,3,0,2,1:T(8,128)S(1)}, s32[]{:T(128)}) while((s32[]{:T(128)}, f32[2,1,32,144]{3,2,1,0:T(8,128)S(1)}, s32[16,4]{0,1:T(4,128)S(1)}, f32[16,2,1,16,128]{4,3,0,2,1:T(8,128)S(1)}, s32[]{:T(128)}) %tuple.138), condition=%wide.while_cond, body=%wide.while_body.sunk | while | flops 2 | bytes 32893 | solution.py:67
  483.1 6.4 collective-permute-done
  500.8 30.0 %while.28 = (s32[]{:T(128)}, f32[2,1,32,144]{3,2,1,0:T(8,128)S(1)}, s32[16,4]{0,1:T(4,128)S(1)}, f32[16,2,1,16,128]{4,3,0,2,1:T(8,128)S(1)}, s32[]{:T(128)}) while((s32[]{:T(128)}, f32[2,1,32,144]{3,2,1,0:T(8,128)S(1)}, s32[16,4]{0,1:T(4,128)S(1)}, f32[16,2,1,16,128]{4,3,0,2,1:T(8,128)S(1)}, s32[]{:T(128)}) %tuple.138), condition=%wide.while_cond, body=%wide.while_body.sunk | while | flops 2 | bytes 32893 | solution.py:67
  534.5 6.4 collective-permute-done
  552.1 30.0 %while.28 = (s32[]{:T(128)}, f32[2,1,32,144]{3,2,1,0:T(8,128)S(1)}, s32[16,4]{0,1:T(4,128)S(1)}, f32[16,2,1,16,128]{4,3,0,2,1:T(8,128)S(1)}, s32[]{:T(128)}) while((s32[]{:T(128)}, f32[2,1,32,144]{3,2,1,0:T(8,128)S(1)}, s32[16,4]{0,1:T(4,128)S(1)}, f32[16,2,1,16,128]{4,3,0,2,1:T(8,128)S(1)}, s32[]{:T(128)}) %tuple.138), condition=%wide.while_cond, body=%wide.while_body.sunk | while | flops 2 | bytes 32893 | solution.py:67
  585.8 6.4 collective-permute-done
  603.5 30.0 %while.28 = (s32[]{:T(128)}, f32[2,1,32,144]{3,2,1,0:T(8,128)S(1)}, s32[16,4]{0,1:T(4,128)S(1)}, f32[16,2,1,16,128]{4,3,0,2,1:T(8,128)S(1)}, s32[]{:T(128)}) while((s32[]{:T(128)}, f32[2,1,32,144]{3,2,1,0:T(8,128)S(1)}, s32[16,4]{0,1:T(4,128)S(1)}, f32[16,2,1,16,128]{4,3,0,2,1:T(8,128)S(1)}, s32[]{:T(128)}) %tuple.138), condition=%wide.while_cond, body=%wide.while_body.sunk | while | flops 2 | bytes 32893 | solution.py:67
  637.2 6.4 collective-permute-done
  654.8 30.0 %while.28 = (s32[]{:T(128)}, f32[2,1,32,144]{3,2,1,0:T(8,128)S(1)}, s32[16,4]{0,1:T(4,128)S(1)}, f32[16,2,1,16,128]{4,3,0,2,1:T(8,128)S(1)}, s32[]{:T(128)}) while((s32[]{:T(128)}, f32[2,1,32,144]{3,2,1,0:T(8,128)S(1)}, s32[16,4]{0,1:T(4,128)S(1)}, f32[16,2,1,16,128]{4,3,0,2,1:T(8,128)S(1)}, s32[]{:T(128)}) %tuple.138), condition=%wide.while_cond, body=%wide.while_body.sunk | while | flops 2 | bytes 32893 | solution.py:67
  688.5 6.4 collective-permute-done
  706.2 30.0 %while.28 = (s32[]{:T(128)}, f32[2,1,32,144]{3,2,1,0:T(8,128)S(1)}, s32[16,4]{0,1:T(4,128)S(1)}, f32[16,2,1,16,128]{4,3,0,2,1:T(8,128)S(1)}, s32[]{:T(128)}) while((s32[]{:T(128)}, f32[2,1,32,144]{3,2,1,0:T(8,128)S(1)}, s32[16,4]{0,1:T(4,128)S(1)}, f32[16,2,1,16,128]{4,3,0,2,1:T(8,128)S(1)}, s32[]{:T(128)}) %tuple.138), condition=%wide.while_cond, body=%wide.while_body.sunk | while | flops 2 | bytes 32893 | solution.py:67
  739.9 6.4 collective-permute-done
  757.6 30.0 %while.28 = (s32[]{:T(128)}, f32[2,1,32,144]{3,2,1,0:T(8,128)S(1)}, s32[16,4]{0,1:T(4,128)S(1)}, f32[16,2,1,16,128]{4,3,0,2,1:T(8,128)S(1)}, s32[]{:T(128)}) while((s32[]{:T(128)}, f32[2,1,32,144]{3,2,1,0:T(8,128)S(1)}, s32[16,4]{0,1:T(4,128)S(1)}, f32[16,2,1,16,128]{4,3,0,2,1:T(8,128)S(1)}, s32[]{:T(128)}) %tuple.138), condition=%wide.while_cond, body=%wide.while_body.sunk | while | flops 2 | bytes 32893 | solution.py:67
  791.3 6.4 collective-permute-done
  808.9 30.0 %while.28 = (s32[]{:T(128)}, f32[2,1,32,144]{3,2,1,0:T(8,128)S(1)}, s32[16,4]{0,1:T(4,128)S(1)}, f32[16,2,1,16,128]{4,3,0,2,1:T(8,128)S(1)}, s32[]{:T(128)}) while((s32[]{:T(128)}, f32[2,1,32,144]{3,2,1,0:T(8,128)S(1)}, s32[16,4]{0,1:T(4,128)S(1)}, f32[16,2,1,16,128]{4,3,0,2,1:T(8,128)S(1)}, s32[]{:T(128)}) %tuple.138), condition=%wide.while_cond, body=%wide.while_body.sunk | while | flops 2 | bytes 32893 | solution.py:67
  842.6 6.4 collective-permute-done
  860.3 30.0 %while.28 = (s32[]{:T(128)}, f32[2,1,32,144]{3,2,1,0:T(8,128)S(1)}, s32[16,4]{0,1:T(4,128)S(1)}, f32[16,2,1,16,128]{4,3,0,2,1:T(8,128)S(1)}, s32[]{:T(128)}) while((s32[]{:T(128)}, f32[2,1,32,144]{3,2,1,0:T(8,128)S(1)}, s32[16,4]{0,1:T(4,128)S(1)}, f32[16,2,1,16,128]{4,3,0,2,1:T(8,128)S(1)}, s32[]{:T(128)}) %tuple.138), condition=%wide.while_cond, body=%wide.while_body.sunk | while | flops 2 | bytes 32893 | solution.py:67
  911.6 30.0 %while.28 = (s32[]{:T(128)}, f32[2,1,32,144]{3,2,1,0:T(8,128)S(1)}, s32[16,4]{0,1:T(4,128)S(1)}, f32[16,2,1,16,128]{4,3,0,2,1:T(8,128)S(1)}, s32[]{:T(128)}) while((s32[]{:T(128)}, f32[2,1,32,144]{3,2,1,0:T(8,128)S(1)}, s32[16,4]{0,1:T(4,128)S(1)}, f32[16,2,1,16,128]{4,3,0,2,1:T(8,128)S(1)}, s32[]{:T(128)}) %tuple.138), condition=%wide.while_cond, body=%wide.while_body.sunk | while | flops 2 | bytes 32893 | solution.py:67
  963.0 30.0 %while.28 = (s32[]{:T(128)}, f32[2,1,32,144]{3,2,1,0:T(8,128)S(1)}, s32[16,4]{0,1:T(4,128)S(1)}, f32[16,2,1,16,128]{4,3,0,2,1:T(8,128)S(1)}, s32[]{:T(128)}) while((s32[]{:T(128)}, f32[2,1,32,144]{3,2,1,0:T(8,128)S(1)}, s32[16,4]{0,1:T(4,128)S(1)}, f32[16,2,1,16,128]{4,3,0,2,1:T(8,128)S(1)}, s32[]{:T(128)}) %tuple.138), condition=%wide.while_cond, body=%wide.while_body.sunk | while | flops 2 | bytes 32893 | solution.py:67
  1014.4 30.0 %while.28 = (s32[]{:T(128)}, f32[2,1,32,144]{3,2,1,0:T(8,128)S(1)}, s32[16,4]{0,1:T(4,128)S(1)}, f32[16,2,1,16,128]{4,3,0,2,1:T(8,128)S(1)}, s32[]{:T(128)}) while((s32[]{:T(128)}, f32[2,1,32,144]{3,2,1,0:T(8,128)S(1)}, s32[16,4]{0,1:T(4,128)S(1)}, f32[16,2,1,16,128]{4,3,0,2,1:T(8,128)S(1)}, s32[]{:T(128)}) %tuple.138), condition=%wide.while_cond, body=%wide.while_body.sunk | while | flops 2 | bytes 32893 | solution.py:67
  1065.7 30.0 %while.28 = (s32[]{:T(128)}, f32[2,1,32,144]{3,2,1,0:T(8,128)S(1)}, s32[16,4]{0,1:T(4,128)S(1)}, f32[16,2,1,16,128]{4,3,0,2,1:T(8,128)S(1)}, s32[]{:T(128)}) while((s32[]{:T(128)}, f32[2,1,32,144]{3,2,1,0:T(8,128)S(1)}, s32[16,4]{0,1:T(4,128)S(1)}, f32[16,2,1,16,128]{4,3,0,2,1:T(8,128)S(1)}, s32[]{:T(128)}) %tuple.138), condition=%wide.while_cond, body=%wide.while_body.sunk | while | flops 2 | bytes 32893 | solution.py:67
  1117.1 30.0 %while.28 = (s32[]{:T(128)}, f32[2,1,32,144]{3,2,1,0:T(8,128)S(1)}, s32[16,4]{0,1:T(4,128)S(1)}, f32[16,2,1,16,128]{4,3,0,2,1:T(8,128)S(1)}, s32[]{:T(128)}) while((s32[]{:T(128)}, f32[2,1,32,144]{3,2,1,0:T(8,128)S(1)}, s32[16,4]{0,1:T(4,128)S(1)}, f32[16,2,1,16,128]{4,3,0,2,1:T(8,128)S(1)}, s32[]{:T(128)}) %tuple.138), condition=%wide.while_cond, body=%wide.while_body.sunk | while | flops 2 | bytes 32893 | solution.py:67
  1168.4 30.0 %while.28 = (s32[]{:T(128)}, f32[2,1,32,144]{3,2,1,0:T(8,128)S(1)}, s32[16,4]{0,1:T(4,128)S(1)}, f32[16,2,1,16,128]{4,3,0,2,1:T(8,128)S(1)}, s32[]{:T(128)}) while((s32[]{:T(128)}, f32[2,1,32,144]{3,2,1,0:T(8,128)S(1)}, s32[16,4]{0,1:T(4,128)S(1)}, f32[16,2,1,16,128]{4,3,0,2,1:T(8,128)S(1)}, s32[]{:T(128)}) %tuple.138), condition=%wide.while_cond, body=%wide.while_body.sunk | while | flops 2 | bytes 32893 | solution.py:67
  1219.8 30.0 %while.28 = (s32[]{:T(128)}, f32[2,1,32,144]{3,2,1,0:T(8,128)S(1)}, s32[16,4]{0,1:T(4,128)S(1)}, f32[16,2,1,16,128]{4,3,0,2,1:T(8,128)S(1)}, s32[]{:T(128)}) while((s32[]{:T(128)}, f32[2,1,32,144]{3,2,1,0:T(8,128)S(1)}, s32[16,4]{0,1:T(4,128)S(1)}, f32[16,2,1,16,128]{4,3,0,2,1:T(8,128)S(1)}, s32[]{:T(128)}) %tuple.138), condition=%wide.while_cond, body=%wide.while_body.sunk | while | flops 2 | bytes 32893 | solution.py:67
  1271.2 30.0 %while.28 = (s32[]{:T(128)}, f32[2,1,32,144]{3,2,1,0:T(8,128)S(1)}, s32[16,4]{0,1:T(4,128)S(1)}, f32[16,2,1,16,128]{4,3,0,2,1:T(8,128)S(1)}, s32[]{:T(128)}) while((s32[]{:T(128)}, f32[2,1,32,144]{3,2,1,0:T(8,128)S(1)}, s32[16,4]{0,1:T(4,128)S(1)}, f32[16,2,1,16,128]{4,3,0,2,1:T(8,128)S(1)}, s32[]{:T(128)}) %tuple.138), condition=%wide.while_cond, body=%wide.while_body.sunk | while | flops 2 | bytes 32893 | solution.py:67
  1322.5 30.0 %while.28 = (s32[]{:T(128)}, f32[2,1,32,144]{3,2,1,0:T(8,128)S(1)}, s32[16,4]{0,1:T(4,128)S(1)}, f32[16,2,1,16,128]{4,3,0,2,1:T(8,128)S(1)}, s32[]{:T(128)}) while((s32[]{:T(128)}, f32[2,1,32,144]{3,2,1,0:T(8,128)S(1)}, s32[16,4]{0,1:T(4,128)S(1)}, f32[16,2,1,16,128]{4,3,0,2,1:T(8,128)S(1)}, s32[]{:T(128)}) %tuple.138), condition=%wide.while_cond, body=%wide.while_body.sunk | while | flops 2 | bytes 32893 | solution.py:67
  1373.9 30.0 %while.28 = (s32[]{:T(128)}, f32[2,1,32,144]{3,2,1,0:T(8,128)S(1)}, s32[16,4]{0,1:T(4,128)S(1)}, f32[16,2,1,16,128]{4,3,0,2,1:T(8,128)S(1)}, s32[]{:T(128)}) while((s32[]{:T(128)}, f32[2,1,32,144]{3,2,1,0:T(8,128)S(1)}, s32[16,4]{0,1:T(4,128)S(1)}, f32[16,2,1,16,128]{4,3,0,2,1:T(8,128)S(1)}, s32[]{:T(128)}) %tuple.138), condition=%wide.while_cond, body=%wide.while_body.sunk | while | flops 2 | bytes 32893 | solution.py:67
  1425.2 30.0 %while.28 = (s32[]{:T(128)}, f32[2,1,32,144]{3,2,1,0:T(8,128)S(1)}, s32[16,4]{0,1:T(4,128)S(1)}, f32[16,2,1,16,128]{4,3,0,2,1:T(8,128)S(1)}, s32[]{:T(128)}) while((s32[]{:T(128)}, f32[2,1,32,144]{3,2,1,0:T(8,128)S(1)}, s32[16,4]{0,1:T(4,128)S(1)}, f32[16,2,1,16,128]{4,3,0,2,1:T(8,128)S(1)}, s32[]{:T(128)}) %tuple.138), condition=%wide.while_cond, body=%wide.while_body.sunk | while | flops 2 | bytes 32893 | solution.py:67
  1476.6 30.0 %while.28 = (s32[]{:T(128)}, f32[2,1,32,144]{3,2,1,0:T(8,128)S(1)}, s32[16,4]{0,1:T(4,128)S(1)}, f32[16,2,1,16,128]{4,3,0,2,1:T(8,128)S(1)}, s32[]{:T(128)}) while((s32[]{:T(128)}, f32[2,1,32,144]{3,2,1,0:T(8,128)S(1)}, s32[16,4]{0,1:T(4,128)S(1)}, f32[16,2,1,16,128]{4,3,0,2,1:T(8,128)S(1)}, s32[]{:T(128)}) %tuple.138), condition=%wide.while_cond, body=%wide.while_body.sunk | while | flops 2 | bytes 32893 | solution.py:67
  1528.0 30.0 %while.28 = (s32[]{:T(128)}, f32[2,1,32,144]{3,2,1,0:T(8,128)S(1)}, s32[16,4]{0,1:T(4,128)S(1)}, f32[16,2,1,16,128]{4,3,0,2,1:T(8,128)S(1)}, s32[]{:T(128)}) while((s32[]{:T(128)}, f32[2,1,32,144]{3,2,1,0:T(8,128)S(1)}, s32[16,4]{0,1:T(4,128)S(1)}, f32[16,2,1,16,128]{4,3,0,2,1:T(8,128)S(1)}, s32[]{:T(128)}) %tuple.138), condition=%wide.while_cond, body=%wide.while_body.sunk | while | flops 2 | bytes 32893 | solution.py:67
  1579.3 30.0 %while.28 = (s32[]{:T(128)}, f32[2,1,32,144]{3,2,1,0:T(8,128)S(1)}, s32[16,4]{0,1:T(4,128)S(1)}, f32[16,2,1,16,128]{4,3,0,2,1:T(8,128)S(1)}, s32[]{:T(128)}) while((s32[]{:T(128)}, f32[2,1,32,144]{3,2,1,0:T(8,128)S(1)}, s32[16,4]{0,1:T(4,128)S(1)}, f32[16,2,1,16,128]{4,3,0,2,1:T(8,128)S(1)}, s32[]{:T(128)}) %tuple.138), condition=%wide.while_cond, body=%wide.while_body.sunk | while | flops 2 | bytes 32893 | solution.py:67
  1630.7 30.0 %while.28 = (s32[]{:T(128)}, f32[2,1,32,144]{3,2,1,0:T(8,128)S(1)}, s32[16,4]{0,1:T(4,128)S(1)}, f32[16,2,1,16,128]{4,3,0,2,1:T(8,128)S(1)}, s32[]{:T(128)}) while((s32[]{:T(128)}, f32[2,1,32,144]{3,2,1,0:T(8,128)S(1)}, s32[16,4]{0,1:T(4,128)S(1)}, f32[16,2,1,16,128]{4,3,0,2,1:T(8,128)S(1)}, s32[]{:T(128)}) %tuple.138), condition=%wide.while_cond, body=%wide.while_body.sunk | while | flops 2 | bytes 32893 | solution.py:67
  1682.0 30.0 %while.28 = (s32[]{:T(128)}, f32[2,1,32,144]{3,2,1,0:T(8,128)S(1)}, s32[16,4]{0,1:T(4,128)S(1)}, f32[16,2,1,16,128]{4,3,0,2,1:T(8,128)S(1)}, s32[]{:T(128)}) while((s32[]{:T(128)}, f32[2,1,32,144]{3,2,1,0:T(8,128)S(1)}, s32[16,4]{0,1:T(4,128)S(1)}, f32[16,2,1,16,128]{4,3,0,2,1:T(8,128)S(1)}, s32[]{:T(128)}) %tuple.138), condition=%wide.while_cond, body=%wide.while_body.sunk | while | flops 2 | bytes 32893 | solution.py:67
  (2779 shorter events, 1618.3 us)
Async XLA Ops:
  0.8 7.3 collective-permute-start.3
  12.7 13.0 collective-permute-start
  29.9 6.2 collective-permute-start.2
  68.5 10.0 collective-permute-start
  119.9 10.0 collective-permute-start
  171.2 10.0 collective-permute-start
  183.9 6.2 collective-permute-start.2
  222.6 10.1 collective-permute-start
  235.3 6.2 collective-permute-start.2
  274.0 10.0 collective-permute-start
  286.7 6.2 collective-permute-start.2
  325.4 10.0 collective-permute-start
  376.7 10.0 collective-permute-start
  428.1 10.0 collective-permute-start
  440.8 6.2 collective-permute-start.2
  479.4 10.0 collective-permute-start
  530.8 10.0 collective-permute-start
  582.2 10.0 collective-permute-start
  594.9 6.2 collective-permute-start.2
  633.5 10.0 collective-permute-start
  646.2 6.2 collective-permute-start.2
  684.9 10.0 collective-permute-start
  736.2 10.0 collective-permute-start
  787.6 10.0 collective-permute-start
  800.3 6.2 collective-permute-start.2
  839.0 10.0 collective-permute-start
  890.3 10.0 collective-permute-start
  941.7 10.0 collective-permute-start
  954.4 6.2 collective-permute-start.2
  993.0 10.0 collective-permute-start
  1044.4 10.0 collective-permute-start
  1095.8 10.0 collective-permute-start
  1108.5 6.2 collective-permute-start.2
  1147.1 10.0 collective-permute-start
  1198.5 10.0 collective-permute-start
  1249.9 10.0 collective-permute-start
  1262.6 6.2 collective-permute-start.2
  1301.2 10.0 collective-permute-start
  1352.6 10.0 collective-permute-start
  1403.9 10.0 collective-permute-start
  1416.6 6.2 collective-permute-start.2
  1455.3 10.0 collective-permute-start
  1506.7 10.0 collective-permute-start
  1558.0 10.0 collective-permute-start
  1570.7 6.2 collective-permute-start.2
  1609.4 10.0 collective-permute-start
  1622.1 6.2 collective-permute-start.2
  1660.7 10.0 collective-permute-start
  (121 other events, 333.9 us)
where the time goes:
time: 1740 us; the launch traced here: 1710 us
  local copies, waits for them, and re-layouts  1020 us (59%)
  waiting for transfers between devices  316 us (18%)
  starting transfers between devices  218 us (13%)
  other arithmetic  148 us (9%)
    gather x1584, local copies, waits for them, and re-layouts  988 us
    ppermute x33, waiting for transfers between devices, shifted_2(): return lax.ppermute(block, axis, route)  208 us
    ppermute x34, waiting for transfers between devices, with_halo(): before = lax.ppermute(last, axis, up)  107 us
    ppermute x34, starting transfers between devices, with_halo(): before = lax.ppermute(last, axis, up)  80.9 us
    ppermute x34, starting transfers between devices, with_halo(): after = lax.ppermute(leading, axis, down)  68.9 us
    ppermute x33, starting transfers between devices, shifted_2(): return lax.ppermute(block, axis, route)  68.6 us
    convert_element_type x66, other arithmetic, within_mesh(): return ((row_ids >= 0) & (row_ids < grid_rows)).astype(jnp.float32)[:, None]  38.8 us
  transfers between devices with their start and end apart: 101, of which 67 were waited for; matrix products, arithmetic and copies ran while one was open for 4% of the time, Pallas kernels for 0%

commit v1 on v0

v1 whole, which is shorter than its diff:
```python
import jax
import jax.numpy as jnp
from jax import lax
from jax.experimental import pallas as pl
from jax.experimental.pallas import tpu as pltpu
from jax.sharding import PartitionSpec as P

MESH = pl.DeviceIdType.MESH

OFF_Y = 8
TAPS = ((0, 0), (-4, 0), (-3, 0), (-2, 0), (-1, 0), (1, 0), (2, 0), (3, 0), (4, 0), (0, -2), (0, -1), (0, 1), (0, 2))
REACH = 4

LEVELS = 24
SLOTS = LEVELS // 2
ROWS = 32
BLOCKS = 8
HALF = 16
GRID = 256

UNITS = [ROWS // 8 + LEVELS - 1 - i for i in range(LEVELS)]
UNIT_BASE = [sum(UNITS[:i]) for i in range(LEVELS + 1)]
X_ROWS = [ROWS + 2 * REACH * (LEVELS - m) for m in range(LEVELS + 1)]
X_BASE = [sum(X_ROWS[:m]) for m in range(LEVELS + 1)]
BIN_PAD = REACH * LEVELS
BIN_ROWS = ROWS + 2 * BIN_PAD
GATHER = 6
CHUNK = 7


def stage_of(y):
    return jnp.minimum((y + 1) // 2, 3)


def stage_end(s):
    return jnp.where(s == 3, 32, 8 * s + 4)


def first_level(s):
    return jnp.where(s == 0, 16, jnp.where(s == 3, 0, 8))


def reach_blocks(s):
    return jnp.where(s == 3, 3, 2)


def worker(s, p, b):
    return 4 * (jnp.maximum(2 * s - 1, 0) + p // 2) + p % 2, 2 * b + jnp.where(s == 0, 1, 0)


def halo_blocks(q):
    return (REACH * (LEVELS - 1 - 2 * q) + HALF - 1) // HALF


def both(*conditions):
    out = conditions[0]
    for c in conditions[1:]:
        out = jnp.logical_and(out, c)
    return out


def chain_kernel(
    surf_ref, tab_ref, bins_ref, out_s, out_r,
    x_all, coef, bins_all, tab8, surf, im_s, im_r,
    bin_send, bin_recv, surf_send, surf_recv, hop_send, hop_recv, im_send, ims_recv, imr_recv, hello,
):
    d, j = lax.axis_index("depth"), lax.axis_index("xline")
    y, zh, bj, core = d // 4, d % 4, j // 2, j % 2
    so = stage_of(y)
    qo = d - stage_end(so) + SLOTS
    ho = halo_blocks(qo)
    sw = jnp.where(core == 1, 0, (y + 1) // 2)
    yw = y - jnp.maximum(2 * sw - 1, 0)
    is_w = both(zh <= 1, jnp.where(core == 1, y <= 1, both(y >= 1, y <= 6)))
    p, b = 2 * yw + zh, bj
    i0 = first_level(sw)
    q0 = i0 // 2
    ew = stage_end(sw)
    is_surf = both(y <= 1, zh <= 1)

    def me(target):
        return both(target[0] == d, target[1] == j)

    def other(target):
        return jnp.logical_not(me(target))

    def inside(block):
        return both(block >= 0, block < BLOCKS)

    def row_inside(jj):
        return both(jj >= 0, jj < 2 * BLOCKS)

    def bin_targets():
        for pp in range(4):
            for db in (0, -1, 1, -2, 2, -3, 3):
                bb = bj + db
                near = both(j >= 2 * bb - ho, j <= 2 * bb + 1 + ho)
                yield pp, db, bb, both(inside(bb), near), worker(so, pp, bb)

    def surf_targets():
        for db in (0, -1, 1):
            bb = bj + db
            yield db, bb, both(is_surf, inside(bb)), (d, 2 * bb + 1)

    def stage_targets(s, on):
        for db in (0, -1, 1, -2, 2, -3, 3):
            bb = b + db
            yield db, bb, both(on, inside(bb), abs(db) <= reach_blocks(jnp.maximum(s, sw))), worker(s, p, bb)

    is_later = both(is_w, sw >= 1)
    is_earlier = both(is_w, sw <= 2)

    barrier = pltpu.get_barrier_semaphore()

    def greet(target):
        pl.semaphore_signal(barrier, inc=1, device_id=target, device_id_type=MESH)

    @pl.when(is_w)
    def _():
        for g in range(6):
            source = (d, 2 * b - 2 + g)

            @pl.when(both(sw == 0, row_inside(source[1]), other(source)))
            def _():
                greet(source)

        def slot(q, c):
            h = halo_blocks(q)
            for g in range(2 * BIN_PAD // HALF + 2):
                source = (ew - SLOTS + q, 2 * b - 6 + g)

                @pl.when(both(row_inside(source[1]), g - 6 >= -h, g - 6 <= 1 + h, other(source)))
                def _():
                    greet(source)

            return c

        lax.fori_loop(q0, SLOTS, slot, 0)
        for db, bb, on, target in stage_targets(sw + 1, is_earlier):

            @pl.when(on)
            def _():
                greet(target)

    for part in range(2):
        block = surf_ref[jnp.minimum(y, 1), part, jnp.minimum(zh, 1)]
        surf[part] = block if part == 0 else jnp.where(y == 1, -block, block)
    zeros8 = jnp.zeros((2, OFF_Y, 128), jnp.float32)
    for f in range(2):

        @pl.when(j == 0)
        def _():
            im_r[f, :, 0:8, :] = zeros8

        @pl.when(j == 2 * BLOCKS - 1)
        def _():
            im_r[f, :, 24:32, :] = zeros8

    def x_row(level):
        base = level * (ROWS + 2 * REACH * LEVELS) - REACH * level * (level - 1)
        return pl.multiple_of(base, 8), pl.multiple_of(REACH * (LEVELS - level), 8)

    @pl.when(is_w)
    def _():
        f = p % 2
        for t in range(2 * len(TAPS)):
            tab8[t] = jnp.broadcast_to(tab_ref[t // 2, t % 2, pl.ds(f, 1), :], (8, 128))
        base, own = x_row(i0)
        zf = jnp.zeros((2, HALF, 128), jnp.float32)
        zi = jnp.zeros((2, HALF, 128), jnp.int32)
        for g in range(2 * BIN_PAD // HALF + 2):
            jj = 2 * b - 6 + g

            @pl.when(jnp.logical_not(row_inside(jj)))
            def _():
                def clear(q, c):
                    bins_all[q, :, pl.ds(HALF * g, HALF), :] = zi
                    return c

                lax.fori_loop(q0, SLOTS, clear, 0)
                row = own + HALF * (g - 6)

                @pl.when(both(row >= 0, HALF * (g - 6) < ROWS + own))
                def _():
                    x_all[:, pl.ds(pl.multiple_of(base + row, 8), HALF), :] = zf

    waits = jnp.int32(0)
    for pp, db, bb, on, target in bin_targets():
        waits += jnp.where(both(on, other(target)), 1, 0)
    for db, bb, on, target in surf_targets():
        waits += jnp.where(both(on, other(target)), 1, 0)
    for db, bb, on, target in stage_targets(sw - 1, is_later):
        waits += jnp.where(on, 1, 0)
    pl.semaphore_wait(barrier, waits)

    def surf_copy(db, bb, target):
        row = X_BASE[16] + 32 + HALF * (j - 2 * bb)
        return pltpu.make_async_remote_copy(
            src_ref=surf, dst_ref=x_all.at[:, pl.ds(pl.multiple_of(row, 8), HALF), :],
            send_sem=surf_send.at[db + 1], recv_sem=surf_recv.at[j - 2 * bb + 2],
            device_id=target, device_id_type=MESH)

    for db, bb, on, target in surf_targets():

        @pl.when(both(on, other(target)))
        def _():
            surf_copy(db, bb, target).start()

        @pl.when(both(on, me(target)))
        def _():
            row = X_BASE[16] + 32 + HALF * (j - 2 * bb)
            x_all[:, pl.ds(pl.multiple_of(row, 8), HALF), :] = surf[...]

    def bin_copy(pp, db, bb, target):
        g = j - 2 * bb + 6
        return pltpu.make_async_remote_copy(
            src_ref=bins_ref.at[0], dst_ref=bins_all.at[qo, :, pl.ds(pl.multiple_of(HALF * g, HALF), HALF), :],
            send_sem=bin_send.at[pp, db + 3], recv_sem=bin_recv.at[qo, g],
            device_id=target, device_id_type=MESH)

    for pp, db, bb, on, target in bin_targets():

        @pl.when(both(on, other(target)))
        def _():
            bin_copy(pp, db, bb, target).start()

        @pl.when(both(on, me(target)))
        def _():
            g = j - 2 * bb + 6
            bins_all[qo, :, pl.ds(pl.multiple_of(HALF * g, HALF), HALF), :] = bins_ref[0]

    for db, bb, on, target in stage_targets(sw - 1, is_later):

        @pl.when(on)
        def _():
            pl.semaphore_signal(hello, inc=1, device_id=target, device_id_type=MESH)

    def hop_copy(db, bb, target):
        base, own = x_row(first_level(sw + 1))
        row = base + own - ROWS * db
        return pltpu.make_async_remote_copy(
            src_ref=x_all.at[:, pl.ds(X_BASE[LEVELS], ROWS), :],
            dst_ref=x_all.at[:, pl.ds(pl.multiple_of(row, 8), ROWS), :],
            send_sem=hop_send.at[db + 3], recv_sem=hop_recv.at[3 - db],
            device_id=target, device_id_type=MESH)

    def image_copy(src, dst, q, k, recv, target):
        return pltpu.make_async_remote_copy(
            src_ref=src, dst_ref=dst, send_sem=im_send.at[q, k], recv_sem=recv,
            device_id=target, device_id_type=MESH)

    def image_targets(q):
        row = X_BASE[2 * q + 2] + REACH * (LEVELS - 2 * q - 2)
        dd = ew - SLOTS + q
        yield 0, 0, p < 2, (dd, 2 * b), row, 16, 0, 0
        yield 0, 1, p < 2, (dd, 2 * b + 1), row + 16, 16, 0, 0
        yield 1, 0, p >= 2, (dd, 2 * b), row, 24, 8, 0
        yield 1, 1, p >= 2, (dd, 2 * b + 1), row + 8, 24, 0, 0
        yield 1, 2, both(p >= 2, b > 0), (dd, 2 * b - 1), row, 8, 24, 1
        yield 1, 3, both(p >= 2, b < BLOCKS - 1), (dd, 2 * b + 2), row + 24, 8, 0, 1

    def image_refs(r, row, rows, to, which):
        f = p % 2
        src = x_all.at[:, pl.ds(row, rows), :]
        if r == 0:
            return src, im_s.at[f], ims_recv.at[f]
        return src, im_r.at[f, :, pl.ds(to, rows), :], imr_recv.at[f, which]

    def apply(i):
        n, base, out = UNITS[i], X_BASE[i], X_BASE[i + 1]
        pieces = -(-n // CHUNK)
        cuts = [n * k // pieces for k in range(pieces + 1)]
        for u0, u1 in zip(cuts, cuts[1:]):
            r, rows = 8 * u0, 8 * (u1 - u0)
            unit = 8 * (UNIT_BASE[i] + u0)
            rr = ii = ri = ir = None
            for t, (dy, dx) in enumerate(TAPS):
                cr, ci = coef[2 * t, unit : unit + rows, :], coef[2 * t + 1, unit : unit + rows, :]
                at = base + r + REACH + dy
                fr, fi = x_all[0, at : at + rows, :], x_all[1, at : at + rows, :]
                if dx != 0:
                    fr, fi = pltpu.roll(fr, (-dx) % 128, 1), pltpu.roll(fi, (-dx) % 128, 1)
                if rr is None:
                    rr, ii, ri, ir = cr * fr, ci * fi, cr * fi, ci * fr
                else:
                    rr, ii, ri, ir = rr + cr * fr, ii + ci * fi, ri + cr * fi, ir + ci * fr
            x_all[0, out + r : out + r + rows, :] = rr - ii
            x_all[1, out + r : out + r + rows, :] = ri + ir

    @pl.when(is_w)
    def _():
        lane = lax.broadcasted_iota(jnp.int32, (8, 128), 1)
        sub = lax.broadcasted_iota(jnp.int32, (8, 128), 0)

        def slot(q, c):
            h = halo_blocks(q)
            for g in range(2 * BIN_PAD // HALF + 2):
                source = (ew - SLOTS + q, 2 * b - 6 + g)

                @pl.when(both(row_inside(source[1]), g - 6 >= -h, g - 6 <= 1 + h, other(source)))
                def _():
                    pltpu.make_async_remote_copy(
                        src_ref=bins_ref.at[0], dst_ref=bins_all.at[q, :, pl.ds(HALF * g, HALF), :],
                        send_sem=bin_send.at[0, 0], recv_sem=bin_recv.at[q, g],
                        device_id=source, device_id_type=MESH).wait_recv()

            for step in range(2):
                i = 2 * q + step
                n = ROWS // 8 + LEVELS - 1 - i
                first = (ROWS // 8 + LEVELS - 1) * i - i * (i - 1) // 2

                def group(k, cc):
                    u = jnp.maximum(jnp.minimum(k * GATHER, n - GATHER), 0)
                    for e in range(GATHER):
                        row = REACH + REACH * i + 8 * (u + e)
                        index = bins_all[q, step, pl.ds(row, 8), :]
                        line = ROWS * b - REACH * (LEVELS - 1 - i) + 8 * (u + e) + sub
                        valid = both(line >= 0, line < GRID)
                        to = pl.multiple_of(8 * (first + u + e), 8)
                        for t, (dy, dx) in enumerate(TAPS):
                            keep = valid
                            if dx > 0:
                                keep = both(valid, lane < 128 - dx)
                            elif dx < 0:
                                keep = both(valid, lane >= -dx)
                            for part in range(2):
                                value = jnp.take_along_axis(
                                    tab8[2 * t + part], index, axis=1, mode="promise_in_bounds")
                                coef[2 * t + part, pl.ds(to, 8), :] = jnp.where(keep, value, 0.0)
                    return cc

                lax.fori_loop(0, (n + GATHER - 1) // GATHER, group, 0)
            return c

        lax.fori_loop(q0, SLOTS, slot, 0)

        for g in range(6):
            source = (d, 2 * b - 2 + g)

            @pl.when(both(sw == 0, row_inside(source[1]), other(source)))
            def _():
                pltpu.make_async_remote_copy(
                    src_ref=surf, dst_ref=x_all.at[:, pl.ds(X_BASE[16] + HALF * g, HALF), :],
                    send_sem=surf_send.at[0], recv_sem=surf_recv.at[g],
                    device_id=source, device_id_type=MESH).wait_recv()

        base, own = x_row(i0)
        for db, bb, on, target in stage_targets(sw - 1, is_later):

            @pl.when(on)
            def _():
                row = base + own + ROWS * db
                pltpu.make_async_remote_copy(
                    src_ref=x_all.at[:, pl.ds(X_BASE[LEVELS], ROWS), :],
                    dst_ref=x_all.at[:, pl.ds(pl.multiple_of(row, 8), ROWS), :],
                    send_sem=hop_send.at[0], recv_sem=hop_recv.at[db + 3],
                    device_id=target, device_id_type=MESH).wait_recv()

        for q in range(SLOTS):

            @pl.when(q >= q0)
            def _():
                apply(2 * q)
                apply(2 * q + 1)
                if q == SLOTS - 1:
                    count = jnp.int32(0)
                    for db, bb, on, target in stage_targets(sw + 1, is_earlier):
                        count += jnp.where(on, 1, 0)

                    @pl.when(is_earlier)
                    def _():
                        pl.semaphore_wait(hello, count)

                    for db, bb, on, target in stage_targets(sw + 1, is_earlier):

                        @pl.when(on)
                        def _():
                            hop_copy(db, bb, target).start()

                for r, k, on, target, row, rows, to, which in image_targets(q):
                    src, dst, recv = image_refs(r, row, rows, to, which)

                    @pl.when(both(on, other(target)))
                    def _():
                        image_copy(src, dst, q, k, recv, target).start()

                    @pl.when(both(on, me(target)))
                    def _():
                        dst[...] = src[...]

    def sources(f):
        yield both(True, other(worker(so, f, bj))), im_s.at[f], ims_recv.at[f]
        for odd in range(2):
            mine = core == odd
            yield both(mine, other(worker(so, 2 + f, bj))), im_r.at[f, :, pl.ds(8 - 8 * odd, 24), :], imr_recv.at[f, 0]
            beside = bj + 2 * odd - 1
            yield (both(mine, inside(beside), other(worker(so, 2 + f, beside))),
                   im_r.at[f, :, pl.ds(24 * odd, 8), :], imr_recv.at[f, 1])

    for f in range(2):
        for on, dst, recv in sources(f):

            @pl.when(on)
            def _():
                pltpu.make_async_remote_copy(
                    src_ref=dst, dst_ref=dst, send_sem=im_send.at[0, 0], recv_sem=recv,
                    device_id=(d, j ^ 1), device_id_type=MESH).wait_recv()

    out_s[...] = im_s[...]
    out_r[...] = im_r[...]

    for db, bb, on, target in surf_targets():

        @pl.when(both(on, other(target)))
        def _():
            surf_copy(db, bb, target).wait_send()

    for pp, db, bb, on, target in bin_targets():

        @pl.when(both(on, other(target)))
        def _():
            bin_copy(pp, db, bb, target).wait_send()

    @pl.when(is_w)
    def _():
        for db, bb, on, target in stage_targets(sw + 1, is_earlier):

            @pl.when(on)
            def _():
                hop_copy(db, bb, target).wait_send()

        for q in range(SLOTS):
            for r, k, on, target, row, rows, to, which in image_targets(q):
                src, dst, recv = image_refs(r, row, rows, to, which)

                @pl.when(both(q >= q0, on, other(target)))
                def _():
                    image_copy(src, dst, q, k, recv, target).wait_send()


def image_kernel(offsets, s_ref, r_ref, out_ref):
    lane = lax.broadcasted_iota(jnp.int32, (HALF, 128), 1)
    for h in range(out_ref.shape[1]):
        hy, hx = offsets[h, 0], offsets[h, 1]
        total = None
        for f in range(2):
            for part in range(2):
                moved = r_ref[f, part, pl.ds(OFF_Y + hy, HALF), :]
                moved = pltpu.roll(moved, lax.rem(128 - hx, 128), 1)
                term = s_ref[f, part] * moved
                total = term if total is None else total + term if part == 0 else total - term
        valid = both(lane + hx >= 0, lane + hx < 128)
        out_ref[0, h] = jnp.where(valid, total, 0.0)


def shards(surface_fields, stencil_table, velocity_bins, offset_list):
    vmem = pl.BlockSpec(memory_space=pltpu.VMEM)
    f32 = jnp.float32
    dma = pltpu.SemaphoreType.DMA
    source, receiver = pl.pallas_call(
        chain_kernel,
        out_shape=(jax.ShapeDtypeStruct((2, 2, 16, 128), f32), jax.ShapeDtypeStruct((2, 2, 32, 128), f32)),
        in_specs=[vmem] * 3,
        out_specs=(vmem, vmem),
        scratch_shapes=[
            pltpu.VMEM((2, sum(X_ROWS), 128), f32),
            pltpu.VMEM((2 * len(TAPS), 8 * (UNIT_BASE[LEVELS] + GATHER), 128), f32),
            pltpu.VMEM((SLOTS, 2, BIN_ROWS, 128), jnp.int32),
            pltpu.VMEM((2 * len(TAPS), 8, 128), f32),
            pltpu.VMEM((2, HALF, 128), f32),
            pltpu.VMEM((2, 2, 16, 128), f32),
            pltpu.VMEM((2, 2, 32, 128), f32),
            dma((4, 7)), dma((SLOTS, 14)), dma((3,)), dma((6,)), dma((7,)), dma((7,)),
            dma((SLOTS, 4)), dma((2,)), dma((2, 2)), pltpu.SemaphoreType.REGULAR,
        ],
        compiler_params=pltpu.CompilerParams(
            collective_id=0, has_side_effects=True, vmem_limit_bytes=56 * 2**20),
    )(surface_fields, stencil_table, velocity_bins)
    return pl.pallas_call(
        image_kernel,
        out_shape=jax.ShapeDtypeStruct((1, offset_list.shape[0], HALF, 128), f32),
        in_specs=[pl.BlockSpec(memory_space=pltpu.SMEM), vmem, vmem],
        out_specs=vmem,
    )(offset_list, source, receiver)


def solution(mesh):
    return jax.shard_map(
        shards,
        mesh=mesh,
        in_specs=(P(None, None, None, "xline", None), P(), P("depth", None, "xline", None), P()),
        out_specs=P("depth", None, "xline", None),
        check_vma=False,
    )
```

time: 1740 us -> 70.3 us (0.04)
  the two profiles are of different devices: /device:TPU:34 before, /device:TPU:121 now
where the time goes in v1:
time: 70.3 us; the launch traced here: 70.1 us
  Pallas kernels  68.7 us (98%)
  local copies, waits for them, and re-layouts  1.36 us (2%)
    pallas_call x1, Pallas kernels, shards(): pl.pallas_call(chain_kernel, out_shape=(jax.ShapeDtypeStruct((2, 2, 16, 1...  67 us
    pallas_call x1, Pallas kernels, shards(): pl.pallas_call(image_kernel, out_shape=jax.ShapeDtypeStruct((1, offset_li...  1.74 us

profile of v1, /device:TPU:121, one launch (start us, length us, event | category | flops | bytes accessed | tf_op | source)
XLA Modules:
  0.0 70.1 jit_solution(18060704331471137112)
XLA Ops:
  0.0 1.4 %copy.5.offsets = s32[16,2]{1,0:T(8,128)} copy(s32[16,2]{0,1:T(2,128)} %param.7) | data formatting | bytes 256 | tf_op args[3]
  1.4 67.0 %shard_map.46 = (f32[2,2,16,128]{3,2,1,0:T(8,128)}, f32[2,2,32,128]{3,2,1,0:T(8,128)}) custom-call(f32[2,2,2,16,128]{4,3,2,1,0:T(8,128)} %surf_ref.1, f32[13,2,2,128]{3,2,1,0:T(2,128)} %tab_ref.1, s32[1,2,16,128]{3,2,1,0:T(8,128)} %bins_ref.1), custom_call_target="tpu_custom_call" | custom-call | tf_op jit(solution)/shard_map/pallas_call | solution.py:460
  68.4 1.7 %shard_map.47 = f32[1,16,16,128]{3,2,1,0:T(8,128)} custom-call(s32[16,2]{1,0:T(8,128)} %copy.5.offsets, f32[2,2,16,128]{3,2,1,0:T(8,128)} %get-tuple-element.7.s_ref, f32[2,2,32,128]{3,2,1,0:T(8,128)} %get-tuple-element.8.r_ref), custom_call_target="tpu_custom_call" | custom-call | tf_op jit(solution)/shard_map/pallas_call | solution.py:479

commit v2 on v1

v2 whole, which is shorter than its diff:
```python
import jax
import jax.numpy as jnp
from jax import lax
from jax.experimental import pallas as pl
from jax.experimental.pallas import tpu as pltpu
from jax.sharding import PartitionSpec as P

MESH = pl.DeviceIdType.MESH

OFF_Y = 8
TAPS = ((0, 0), (-4, 0), (-3, 0), (-2, 0), (-1, 0), (1, 0), (2, 0), (3, 0), (4, 0), (0, -2), (0, -1), (0, 1), (0, 2))
REACH = 4

LEVELS = 24
SLOTS = LEVELS // 2
ROWS = 32
BLOCKS = 8
HALF = 16
GRID = 256

UNITS = [ROWS // 8 + LEVELS - 1 - i for i in range(LEVELS)]
UNIT_BASE = [sum(UNITS[:i]) for i in range(LEVELS + 1)]
X_ROWS = [ROWS + 2 * REACH * (LEVELS - m) for m in range(LEVELS + 1)]
X_BASE = [sum(X_ROWS[:m]) for m in range(LEVELS + 1)]
BIN_PAD = REACH * LEVELS
BIN_ROWS = ROWS + 2 * BIN_PAD
GATHER = 6
CHUNK = 7


def stage_of(y):
    return jnp.minimum((y + 1) // 2, 3)


def stage_end(s):
    return jnp.where(s == 3, 32, 8 * s + 4)


def first_level(s):
    return jnp.where(s == 0, 16, jnp.where(s == 3, 0, 8))


def reach_blocks(s):
    return jnp.where(s == 3, 3, 2)


def worker(s, p, b):
    return 4 * (jnp.maximum(2 * s - 1, 0) + p // 2) + p % 2, 2 * b + jnp.where(s == 0, 1, 0)


def halo(level):
    return REACH * (LEVELS - 1 - level)


def sent_halo(q):
    return -(-halo(2 * q) // 8) * 8


def both(*conditions):
    out = conditions[0]
    for c in conditions[1:]:
        out = jnp.logical_and(out, c)
    return out


def chain_kernel(
    surf_ref, tab_hbm, bins_ref, out_s, out_r,
    x_all, coef, bins_all, tab8, tab_ref, zero_rows,
    tab_sem, self_sem, zero_sem, bin_send, bin_recv, edge_send, fwd_send, fwd_recv, surf_send, surf_recv, hop_send, hop_recv,
    im_send, ims_recv, imr_recv, hello,
):
    d, j = lax.axis_index("depth"), lax.axis_index("xline")
    y, zh, bj, core = d // 4, d % 4, j // 2, j % 2
    so = stage_of(y)
    qo = d - stage_end(so) + SLOTS
    sw = jnp.where(core == 1, 0, (y + 1) // 2)
    yw = y - jnp.maximum(2 * sw - 1, 0)
    is_w = both(zh <= 1, jnp.where(core == 1, y <= 1, both(y >= 1, y <= 6)))
    p, b = 2 * yw + zh, bj
    i0 = first_level(sw)
    q0 = i0 // 2
    ew = stage_end(sw)
    is_surf = both(y <= 1, zh <= 1)
    self_slot = both(so == sw, is_w)

    def me(target):
        return both(target[0] == d, target[1] == j)

    def other(target):
        return jnp.logical_not(me(target))

    def inside(block):
        return both(block >= 0, block < BLOCKS)

    def remote(src, dst, send, recv, target):
        return pltpu.make_async_remote_copy(
            src_ref=src, dst_ref=dst, send_sem=send, recv_sem=recv, device_id=target, device_id_type=MESH)

    def surf_targets():
        for db in (0, -1, 1):
            bb = bj + db
            yield db, both(is_surf, inside(bb)), (d, 2 * bb + 1)

    def stage_targets(s, on):
        for db in (0, -1, 1, -2, 2, -3, 3):
            bb = b + db
            near = True if abs(db) <= 2 else reach_blocks(jnp.maximum(s, sw)) == 3
            yield db, both(on, inside(bb), near), worker(s, p, bb)

    SIDES = (-1, 1, -2, 2, -3, 3)

    def beside():
        for e, db in enumerate(SIDES):
            far = 1 if abs(db) == 1 else jnp.where(sw == 0, 0, jnp.where(sw == 3, 1, 1 if abs(db) == 2 else 0))
            yield e, db, both(is_w, inside(b + db), far == 1), worker(sw, p, b + db)

    is_later = both(is_w, sw >= 1)
    is_earlier = both(is_w, sw <= 2)
    edge_block = bj + 2 * core - 1
    edge_on = both(qo == SLOTS - 1, inside(edge_block))

    barrier = pltpu.get_barrier_semaphore()

    def greet(target):
        pl.semaphore_signal(barrier, inc=1, device_id=target, device_id_type=MESH)

    tab_copy = pltpu.make_async_copy(tab_hbm, tab_ref, tab_sem)

    @pl.when(is_w)
    def _():
        tab_copy.start()

        @pl.when(sw == 0)
        def _():
            for g in range(6):
                source = (d, 2 * b - 2 + g)

                @pl.when(both(source[1] >= 0, source[1] < 2 * BLOCKS, g != 3))
                def _():
                    greet(source)

        def slot(q, c):
            mine = both(self_slot, q == qo)

            @pl.when(jnp.logical_not(both(mine, core == 0)))
            def _():
                greet((ew - SLOTS + q, 2 * b))

            @pl.when(jnp.logical_not(both(mine, core == 1)))
            def _():
                greet((ew - SLOTS + q, 2 * b + 1))

            return c

        lax.fori_loop(q0, SLOTS, slot, 0)
        for db, on, target in stage_targets(sw + 1, is_earlier):

            @pl.when(on)
            def _():
                greet(target)

        for e, db, on, target in beside():

            @pl.when(on)
            def _():
                greet(target)

        @pl.when(b > 0)
        def _():
            greet((ew - 1, 2 * b - 1))

        @pl.when(b < BLOCKS - 1)
        def _():
            greet((ew - 1, 2 * b + 2))

    zero_rows[...] = jnp.zeros((2, 2, OFF_Y, 128), jnp.float32)

    def zero_copy():
        return pltpu.make_async_copy(
            zero_rows, out_r.at[:, :, pl.ds(pl.multiple_of(24 * core, 8), OFF_Y), :], zero_sem)

    at_edge = jnp.logical_not(inside(edge_block))

    @pl.when(at_edge)
    def _():
        zero_copy().start()

    def x_row(level):
        base = level * (ROWS + 2 * REACH * LEVELS) - REACH * level * (level - 1)
        return pl.multiple_of(base, 8), pl.multiple_of(REACH * (LEVELS - level), 8)

    count = jnp.int32(0)
    for pp in range(4):
        count += jnp.where(other(worker(so, pp, bj)), 1, 0)
    count += jnp.where(edge_on, 4, 0)
    for db, on, target in surf_targets():
        count += jnp.where(both(on, other(target)), 1, 0)
    for db, on, target in stage_targets(sw - 1, is_later):
        count += jnp.where(on, 1, 0)
    for e, db, on, target in beside():
        count += jnp.where(on, 1, 0)
    pl.semaphore_wait(barrier, count)

    own_rows = pl.multiple_of(BIN_PAD + HALF * core, HALF)

    def bin_copy(pp):
        return remote(bins_ref.at[0], bins_all.at[qo, :, pl.ds(own_rows, HALF), :],
                      bin_send.at[pp], bin_recv.at[qo], worker(so, pp, bj))

    def edge_copy(pp):
        start = pl.multiple_of(8 * core, 8)
        to = pl.multiple_of(jnp.where(core == 1, BIN_PAD - 8, BIN_PAD + ROWS), 8)
        return remote(bins_ref.at[0, :, pl.ds(start, 8), :], bins_all.at[SLOTS - 1, :, pl.ds(to, 8), :],
                      edge_send.at[pp], fwd_recv.at[SLOTS - 1, 1 - core], worker(so, pp, edge_block))

    surf_block = surf_ref.at[jnp.minimum(y, 1), :, jnp.minimum(zh, 1)]

    def surf_row():
        return X_BASE[16] + 32 + HALF * core

    def surf_copy(db, target):
        row = pl.multiple_of(surf_row() - ROWS * db, 8)
        return remote(surf_block, x_all.at[:, pl.ds(row, HALF), :], surf_send.at[db + 1],
                      surf_recv.at[core - 2 * db + 2], target)

    def self_bins():
        return pltpu.make_async_copy(
            bins_ref.at[0], bins_all.at[qo, :, pl.ds(own_rows, HALF), :], self_sem.at[0])

    def self_surf():
        return pltpu.make_async_copy(
            surf_block, x_all.at[:, pl.ds(X_BASE[16] + 32 + HALF, HALF), :], self_sem.at[1])

    for pp in range(4):
        target = worker(so, pp, bj)

        @pl.when(other(target))
        def _():
            bin_copy(pp).start()

        @pl.when(me(target))
        def _():
            self_bins().start()

    @pl.when(edge_on)
    def _():
        for pp in range(4):
            edge_copy(pp).start()

    @pl.when(is_surf)
    def _():
        for db, on, target in surf_targets():

            @pl.when(both(on, other(target)))
            def _():
                surf_copy(db, target).start()

            @pl.when(both(on, me(target)))
            def _():
                self_surf().start()

    @pl.when(is_later)
    def _():
        for db, on, target in stage_targets(sw - 1, is_later):

            @pl.when(on)
            def _():
                pl.semaphore_signal(hello, inc=1, device_id=target, device_id_type=MESH)

    def forwards(q):
        for e, db, on, target in beside():
            rows = min(ROWS, sent_halo(q) - ROWS * (abs(db) - 1))
            if rows > 0:
                start = BIN_PAD if db < 0 else BIN_PAD + ROWS - rows
                src = bins_all.at[q, :, start : start + rows, :]
                to = start - ROWS * db
                dst = bins_all.at[q, :, to : to + rows, :]
                send = fwd_send.at[6 * (q % 4) + e if q < 8 else 24 + 2 * (q - 8) + e]
                yield on, remote(src, dst, send, fwd_recv.at[q, 0 if db > 0 else 1], target)

    def wait_sent(*slots):
        for q in slots:
            for on, copy in forwards(q):

                @pl.when(on)
                def _():
                    copy.wait_send()

    def wait_own(q):
        here = both(self_slot, q == qo)

        @pl.when(jnp.logical_not(here))
        def _():
            dst = bins_all.at[q, :, BIN_PAD : BIN_PAD + ROWS, :]
            remote(dst, dst, bin_send.at[0], bin_recv.at[q], (ew - SLOTS + q, 2 * b)).wait_recv()

        @pl.when(here)
        def _():
            dst = bins_all.at[q, :, pl.ds(pl.multiple_of(BIN_PAD + HALF * (1 - core), HALF), HALF), :]
            remote(dst, dst, bin_send.at[0], bin_recv.at[q], (d, j + 1 - 2 * core)).wait_recv()
            self_bins().wait()

    def forward(*slots):
        for q in slots:
            wait_own(q)
            for on, copy in forwards(q):

                @pl.when(on)
                def _():
                    copy.start()

    def wait_forwarded(*slots):
        for q in slots:
            rows_all = sent_halo(q)
            deepest = -(-rows_all // ROWS)
            for side in range(2):
                there = b if side == 0 else BLOCKS - 1 - b
                for k in range(1, deepest + 1):
                    rows = min(rows_all, ROWS * k)
                    start = BIN_PAD - rows if side == 0 else BIN_PAD + ROWS
                    dst = bins_all.at[q, :, start : start + rows, :]

                    @pl.when(there >= k if k == deepest else there == k)
                    def _():
                        remote(dst, dst, bin_send.at[0], fwd_recv.at[q, side], (d, j + 1 - 2 * core)).wait_recv()

    def hop_copy(db, target):
        base, own = x_row(first_level(sw + 1))
        row = pl.multiple_of(base + own - ROWS * db, 8)
        return remote(x_all.at[:, pl.ds(X_BASE[LEVELS], ROWS), :], x_all.at[:, pl.ds(row, ROWS), :],
                      hop_send.at[db + 3], hop_recv.at[3 - db], target)

    def source_images(q, row):
        dd, f = ew - SLOTS + q, p % 2
        for half in range(2):
            yield half, remote(x_all.at[:, pl.ds(pl.multiple_of(row + HALF * half, 8), HALF), :], out_s.at[f],
                               im_send.at[q % 4, half], ims_recv.at[f], (dd, 2 * b + half))

    def receiver_images(q, row):
        dd, f = ew - SLOTS + q, p % 2
        for half in range(2):
            yield half, remote(x_all.at[:, pl.ds(pl.multiple_of(row + 8 * half, 8), 24), :],
                               out_r.at[f, :, pl.ds(8 - 8 * half, 24), :],
                               im_send.at[q % 4, half], imr_recv.at[f, 0], (dd, 2 * b + half))

    def edge_images(q, row):
        dd, f = ew - SLOTS + q, p % 2
        for half in range(2):
            on = b > 0 if half == 0 else b < BLOCKS - 1
            yield on, remote(x_all.at[:, pl.ds(pl.multiple_of(row + 24 * half, 8), 8), :],
                             out_r.at[f, :, pl.ds(24 - 24 * half, 8), :],
                             im_send.at[q % 4, 2 + half], imr_recv.at[f, 1], (dd, 2 * b - 1 + 3 * half))

    def send_images(q, level):
        base, own = x_row(level) if not isinstance(level, int) else (X_BASE[level], REACH * (LEVELS - level))
        row = base + own
        mine = both(self_slot, q == qo)

        def pair(images, local):
            for half, copy in images(q, row):
                here = both(mine, core == half)

                @pl.when(jnp.logical_not(here))
                def _():
                    copy.start()

                @pl.when(here)
                def _():
                    local(half)

        def local_source(half):
            copy = pltpu.make_async_copy(
                x_all.at[:, pl.ds(pl.multiple_of(row + HALF * half, 8), HALF), :], out_s.at[p % 2], self_sem.at[2])
            copy.start()
            copy.wait()

        def local_receiver(half):
            copy = pltpu.make_async_copy(
                x_all.at[:, pl.ds(pl.multiple_of(row + 8 * half, 8), 24), :],
                out_r.at[p % 2, :, pl.ds(8 - 8 * half, 24), :], self_sem.at[2])
            copy.start()
            copy.wait()

        @pl.when(p < 2)
        def _():
            pair(source_images, local_source)

        @pl.when(p >= 2)
        def _():
            pair(receiver_images, local_receiver)
            for on, copy in edge_images(q, row):

                @pl.when(on)
                def _():
                    copy.start()

    def wait_images(q):
        base, own = x_row(2 * q + 2)
        mine = both(self_slot, q == qo)

        def pair(images):
            for half, copy in images(q, base + own):

                @pl.when(jnp.logical_not(both(mine, core == half)))
                def _():
                    copy.wait_send()

        @pl.when(p < 2)
        def _():
            pair(source_images)

        @pl.when(p >= 2)
        def _():
            pair(receiver_images)
            for on, copy in edge_images(q, base + own):

                @pl.when(on)
                def _():
                    copy.wait_send()

    def apply(i):
        n, base, out = UNITS[i], X_BASE[i], X_BASE[i + 1]
        pieces = -(-n // CHUNK)
        cuts = [n * k // pieces for k in range(pieces + 1)]
        for u0, u1 in zip(cuts, cuts[1:]):
            r, rows = 8 * u0, 8 * (u1 - u0)
            unit = 8 * (UNIT_BASE[i] + u0)
            rr = ii = ri = ir = None
            for t, (dy, dx) in enumerate(TAPS):
                cr, ci = coef[2 * t, unit : unit + rows, :], coef[2 * t + 1, unit : unit + rows, :]
                at = base + r + REACH + dy
                fr, fi = x_all[0, at : at + rows, :], x_all[1, at : at + rows, :]
                if dx != 0:
                    fr, fi = pltpu.roll(fr, (-dx) % 128, 1), pltpu.roll(fi, (-dx) % 128, 1)
                if rr is None:
                    rr, ii, ri, ir = cr * fr, ci * fi, cr * fi, ci * fr
                else:
                    rr, ii, ri, ir = rr + cr * fr, ii + ci * fi, ri + cr * fi, ir + ci * fr
            x_all[0, out + r : out + r + rows, :] = rr - ii
            x_all[1, out + r : out + r + rows, :] = ri + ir

    def look_up(q, size):
        lane = lax.broadcasted_iota(jnp.int32, (8, 128), 1)
        sub = lax.broadcasted_iota(jnp.int32, (8, 128), 0)
        for step in range(2):
            i = 2 * q + step
            n = ROWS // 8 + LEVELS - 1 - i
            first = (ROWS // 8 + LEVELS - 1) * i - i * (i - 1) // 2

            def group(k, c):
                u = jnp.minimum(k * size, n - size)
                for e in range(size):
                    row = REACH + REACH * i + 8 * (u + e)
                    index = bins_all[q, step, pl.ds(row, 8), :]
                    line = ROWS * b - REACH * (LEVELS - 1 - i) + 8 * (u + e) + sub
                    valid = both(line >= 0, line < GRID)
                    to = pl.multiple_of(8 * (first + u + e), 8)
                    for t, (dy, dx) in enumerate(TAPS):
                        keep = valid
                        if dx > 0:
                            keep = both(valid, lane < 128 - dx)
                        elif dx < 0:
                            keep = both(valid, lane >= -dx)
                        for part in range(2):
                            value = jnp.take_along_axis(
                                tab8[2 * t + part], index, axis=1, mode="promise_in_bounds")
                            coef[2 * t + part, pl.ds(to, 8), :] = jnp.where(keep, value, 0.0)
                return c

            lax.fori_loop(0, (n + size - 1) // size, group, 0)

    def look_up_slots(start, end):
        def slot(q, c):
            look_up(q, GATHER)
            return c

        lax.fori_loop(start, end, slot, 0)

    @pl.when(is_w)
    def _():
        f = p % 2
        tab_copy.wait()
        for t in range(2 * len(TAPS)):
            tab8[t] = jnp.broadcast_to(tab_ref[t // 2, t % 2, pl.ds(f, 1), :], (8, 128))
        base, own = x_row(i0)
        zf = jnp.zeros((2, ROWS, 128), jnp.float32)
        zi = jnp.zeros((2, ROWS, 128), jnp.int32)
        for db in SIDES:

            @pl.when(jnp.logical_not(inside(b + db)))
            def _():
                def clear(q, c):
                    bins_all[q, :, pl.ds(BIN_PAD + ROWS * db, ROWS), :] = zi
                    return c

                lax.fori_loop(q0, SLOTS, clear, 0)
                row = own + ROWS * db

                @pl.when(both(row >= 0, ROWS * db < ROWS + own))
                def _():
                    x_all[:, pl.ds(pl.multiple_of(base + row, 8), ROWS), :] = zf

    @pl.when(is_w)
    def _():
        @pl.when(sw >= 1)
        def _():
            forward(4)

        forward(8)

        @pl.when(sw >= 1)
        def _():
            forward(5)

        forward(9)
        wait_forwarded(8)
        look_up_slots(8, 9)

        @pl.when(sw >= 1)
        def _():
            wait_forwarded(4)
            look_up_slots(4, 5)
            forward(6)

        forward(10)
        wait_forwarded(9)

        @pl.when(sw >= 1)
        def _():
            wait_forwarded(5)
            look_up_slots(5, 6)
            forward(7)

            @pl.when(sw == 3)
            def _():
                wait_sent(4, 5, 6, 7)
                forward(0, 1, 2, 3)

        @pl.when(sw == 0)
        def _():
            for g in range(6):
                jj = 2 * b - 2 + g

                @pl.when(both(jj >= 0, jj < 2 * BLOCKS, g != 3))
                def _():
                    dst = x_all.at[:, pl.ds(X_BASE[16] + HALF * g, HALF), :]
                    remote(surf_block, dst, surf_send.at[0], surf_recv.at[g], (d, jj)).wait_recv()

            self_surf().wait()

            @pl.when(p >= 2)
            def _():
                top = slice(X_BASE[16], X_BASE[17])
                x_all[1, top, :] = -x_all[1, top, :]

            apply(16)
            apply(17)

        look_up_slots(9, 10)
        wait_forwarded(10)
        look_up_slots(10, 11)

        @pl.when(sw == 0)
        def _():
            for i in range(18, 22):
                apply(i)

        @pl.when(sw >= 1)
        def _():
            wait_forwarded(6, 7)
            look_up_slots(6, 8)

        wait_own(SLOTS - 1)
        wait_forwarded(SLOTS - 1)
        look_up(SLOTS - 1, 4)

        @pl.when(sw == 3)
        def _():
            wait_forwarded(0, 1, 2, 3)
            look_up_slots(0, 4)

        @pl.when(is_later)
        def _():
            base, own = x_row(i0)
            for db, on, target in stage_targets(sw - 1, is_later):

                @pl.when(on)
                def _():
                    dst = x_all.at[:, pl.ds(pl.multiple_of(base + own + ROWS * db, 8), ROWS), :]
                    remote(dst, dst, hop_send.at[0], hop_recv.at[db + 3], target).wait_recv()

        def slab(q):
            apply(2 * q)
            apply(2 * q + 1)

            @pl.when(sw == 3)
            def _():
                if q >= 4:
                    wait_images(q - 4)
                send_images(q, 2 * q + 2)

        @pl.when(sw == 3)
        def _():
            for q in range(4):
                slab(q)

        @pl.when(sw >= 1)
        def _():
            for q in range(4, SLOTS - 1):
                slab(q)

        slab(SLOTS - 1)

        @pl.when(is_earlier)
        def _():
            words = jnp.int32(0)
            for db, on, target in stage_targets(sw + 1, is_earlier):
                words += jnp.where(on, 1, 0)
            pl.semaphore_wait(hello, words)
            for db, on, target in stage_targets(sw + 1, is_earlier):

                @pl.when(on)
                def _():
                    hop_copy(db, target).start()

            def slot(q, c):
                @pl.when(q - 4 >= q0)
                def _():
                    wait_images(q - 4)

                send_images(q, 2 * q + 2)
                return c

            lax.fori_loop(q0, SLOTS, slot, 0)

    for f in range(2):
        def wait_image(on, dst, recv):
            @pl.when(on)
            def _():
                remote(dst, dst, im_send.at[0, 0], recv, (d, j + 1 - 2 * core)).wait_recv()

        wait_image(other(worker(so, f, bj)), out_s.at[f], ims_recv.at[f])
        wait_image(other(worker(so, 2 + f, bj)), out_r.at[f, :, pl.ds(pl.multiple_of(8 - 8 * core, 8), 24), :],
                   imr_recv.at[f, 0])
        wait_image(inside(edge_block), out_r.at[f, :, pl.ds(pl.multiple_of(24 * core, 8), 8), :], imr_recv.at[f, 1])

    @pl.when(at_edge)
    def _():
        zero_copy().wait()

    for pp in range(4):

        @pl.when(other(worker(so, pp, bj)))
        def _():
            bin_copy(pp).wait_send()

    @pl.when(edge_on)
    def _():
        for pp in range(4):
            edge_copy(pp).wait_send()

    @pl.when(is_surf)
    def _():
        for db, on, target in surf_targets():

            @pl.when(both(on, other(target)))
            def _():
                surf_copy(db, target).wait_send()

    @pl.when(is_w)
    def _():
        @pl.when(sw == 3)
        def _():
            wait_sent(0, 1, 2, 3)

        @pl.when(both(sw >= 1, sw <= 2))
        def _():
            wait_sent(4, 5, 6, 7)

        wait_sent(8, 9, 10)

        @pl.when(is_earlier)
        def _():
            for db, on, target in stage_targets(sw + 1, is_earlier):

                @pl.when(on)
                def _():
                    hop_copy(db, target).wait_send()

        def slot(q, c):
            wait_images(q)
            return c

        lax.fori_loop(SLOTS - 4, SLOTS, slot, 0)


def image_kernel(offsets, s_ref, r_ref, out_ref):
    lane = lax.broadcasted_iota(jnp.int32, (HALF, 128), 1)
    for h in range(out_ref.shape[1]):
        hy, hx = offsets[0, h], offsets[1, h]
        total = None
        for f in range(2):
            for part in range(2):
                moved = r_ref[f, part, pl.ds(OFF_Y + hy, HALF), :]
                moved = pltpu.roll(moved, lax.rem(128 - hx, 128), 1)
                term = s_ref[f, part] * moved
                total = term if total is None else total + term if part == 0 else total - term
        valid = both(lane + hx >= 0, lane + hx < 128)
        out_ref[0, h] = jnp.where(valid, total, 0.0)


def shards(surface_fields, stencil_table, velocity_bins, offset_list):
    vmem = pl.BlockSpec(memory_space=pltpu.VMEM)
    hbm = pl.BlockSpec(memory_space=pl.ANY)
    f32 = jnp.float32
    dma = pltpu.SemaphoreType.DMA
    source, receiver = pl.pallas_call(
        chain_kernel,
        out_shape=(jax.ShapeDtypeStruct((2, 2, 16, 128), f32), jax.ShapeDtypeStruct((2, 2, 32, 128), f32)),
        in_specs=[hbm] * 3,
        out_specs=(hbm, hbm),
        scratch_shapes=[
            pltpu.VMEM((2, sum(X_ROWS), 128), f32),
            pltpu.VMEM((2 * len(TAPS), 8 * (UNIT_BASE[LEVELS] + GATHER), 128), f32),
            pltpu.VMEM((SLOTS, 2, BIN_ROWS, 128), jnp.int32),
            pltpu.VMEM((2 * len(TAPS), 8, 128), f32),
            pltpu.VMEM(stencil_table.shape, f32),
            pltpu.VMEM((2, 2, OFF_Y, 128), f32),
            dma, dma((3,)), dma,
            dma((4,)), dma((SLOTS,)), dma((4,)), dma((30,)), dma((SLOTS, 2)),
            dma((3,)), dma((6,)), dma((7,)), dma((7,)),
            dma((4, 4)), dma((2,)), dma((2, 2)), pltpu.SemaphoreType.REGULAR,
        ],
        compiler_params=pltpu.CompilerParams(
            collective_id=0, has_side_effects=True, vmem_limit_bytes=56 * 2**20),
    )(surface_fields, stencil_table, velocity_bins)
    return pl.pallas_call(
        image_kernel,
        out_shape=jax.ShapeDtypeStruct((1, offset_list.shape[0], HALF, 128), f32),
        in_specs=[pl.BlockSpec(memory_space=pltpu.SMEM), vmem, vmem],
        out_specs=vmem,
    )(offset_list.T, source, receiver)


def solution(mesh):
    return jax.shard_map(
        shards,
        mesh=mesh,
        in_specs=(P(None, None, None, "xline", None), P(), P("depth", None, "xline", None), P()),
        out_specs=P("depth", None, "xline", None),
        check_vma=False,
    )
```

time: 70.3 us -> 63.2 us (0.90)
  the two profiles are of different devices: /device:TPU:121 before, /device:TPU:58 now
where the time goes in v2:
time: 63.2 us; the launch traced here: 63 us
  Pallas kernels  63 us (100%)
    pallas_call x1, Pallas kernels, shards(): pl.pallas_call(chain_kernel, out_shape=(jax.ShapeDtypeStruct((2, 2, 16, 1...  61.3 us
    pallas_call x1, Pallas kernels, shards(): pl.pallas_call(image_kernel, out_shape=jax.ShapeDtypeStruct((1, offset_li...  1.74 us

profile of v2, /device:TPU:58, one launch (start us, length us, event | category | flops | bytes accessed | tf_op | source)
XLA Modules:
  0.0 63.0 jit_solution(35686304153800724)
XLA Ops:
  0.0 61.3 %shard_map.46 = (f32[2,2,16,128]{3,2,1,0:T(8,128)}, f32[2,2,32,128]{3,2,1,0:T(8,128)}) custom-call(f32[2,2,2,16,128]{4,3,2,1,0:T(8,128)} %surf_ref.1, f32[13,2,2,128]{3,2,1,0:T(2,128)} %tab_hbm.1, s32[1,2,16,128]{3,2,1,0:T(8,128)} %bins_ref.1), custom_call_target="tpu_custom_call" | custom-call | tf_op jit(solution)/shard_map/pallas_call | solution.py:717
  61.3 1.7 %shard_map.47 = f32[1,16,16,128]{3,2,1,0:T(8,128)} custom-call(s32[2,16]{1,0:T(2,128)} %bitcast.1, f32[2,2,16,128]{3,2,1,0:T(8,128)} %get-tuple-element.7.s_ref, f32[2,2,32,128]{3,2,1,0:T(8,128)} %get-tuple-element.8.r_ref), custom_call_target="tpu_custom_call" | custom-call | tf_op jit(solution)/shard_map/pallas_call | solution.py:737

commit v3 on v2

--- a/solution.py
+++ b/solution.py
@@ -28,24 +28,25 @@
 CHUNK = 7
 
 
-def stage_of(y):
-    return jnp.minimum((y + 1) // 2, 3)
+def pick(s, *values):
+    return jnp.where(s == 0, values[0], jnp.where(s == 1, values[1], jnp.where(s == 2, values[2], values[3])))
+
+
+def stage_of(d):
+    return jnp.where(d < 4, 0, jnp.where(d < 12, 1, jnp.where(d < 20, 2, 3)))
 
 
 def stage_end(s):
-    return jnp.where(s == 3, 32, 8 * s + 4)
+    return pick(s, 4, 12, 20, 32)
 
 
 def first_level(s):
-    return jnp.where(s == 0, 16, jnp.where(s == 3, 0, 8))
-
-
-def reach_blocks(s):
-    return jnp.where(s == 3, 3, 2)
+    return pick(s, 16, 8, 8, 0)
 
 
 def worker(s, p, b):
-    return 4 * (jnp.maximum(2 * s - 1, 0) + p // 2) + p % 2, 2 * b + jnp.where(s == 0, 1, 0)
+    plane = jnp.where(s <= 1, p >> 1, 7 - 5 * (p >> 1))
+    return 4 * plane + (p & 1), 2 * b + pick(s, 1, 0, 0, 1)
 
 
 def halo(level):
@@ -70,15 +71,15 @@
     im_send, ims_recv, imr_recv, hello,
 ):
     d, j = lax.axis_index("depth"), lax.axis_index("xline")
-    y, zh, bj, core = d // 4, d % 4, j // 2, j % 2
-    so = stage_of(y)
+    y, zh, bj, core = d >> 2, d & 3, j >> 1, j & 1
+    so = stage_of(d)
     qo = d - stage_end(so) + SLOTS
-    sw = jnp.where(core == 1, 0, (y + 1) // 2)
-    yw = y - jnp.maximum(2 * sw - 1, 0)
-    is_w = both(zh <= 1, jnp.where(core == 1, y <= 1, both(y >= 1, y <= 6)))
+    sw = jnp.where(y <= 1, 1 - core, 2 + core)
+    yw = jnp.where(both(y >= 1, y <= 2), 1, 0)
+    is_w = both(zh <= 1, jnp.where(y == 7, True, y <= 2))
     p, b = 2 * yw + zh, bj
     i0 = first_level(sw)
-    q0 = i0 // 2
+    q0 = i0 >> 1
     ew = stage_end(sw)
     is_surf = both(y <= 1, zh <= 1)
     self_slot = both(so == sw, is_w)
@@ -104,15 +105,15 @@
     def stage_targets(s, on):
         for db in (0, -1, 1, -2, 2, -3, 3):
             bb = b + db
-            near = True if abs(db) <= 2 else reach_blocks(jnp.maximum(s, sw)) == 3
+            near = True if abs(db) <= 2 else jnp.maximum(s, sw) == 3
             yield db, both(on, inside(bb), near), worker(s, p, bb)
 
     SIDES = (-1, 1, -2, 2, -3, 3)
 
     def beside():
         for e, db in enumerate(SIDES):
-            far = 1 if abs(db) == 1 else jnp.where(sw == 0, 0, jnp.where(sw == 3, 1, 1 if abs(db) == 2 else 0))
-            yield e, db, both(is_w, inside(b + db), far == 1), worker(sw, p, b + db)
+            near = sw >= (0, 1, 3)[abs(db) - 1]
+            yield e, db, both(is_w, inside(b + db), near), worker(sw, p, b + db)
 
     is_later = both(is_w, sw >= 1)
     is_earlier = both(is_w, sw <= 2)
@@ -275,7 +276,7 @@
                 src = bins_all.at[q, :, start : start + rows, :]
                 to = start - ROWS * db
                 dst = bins_all.at[q, :, to : to + rows, :]
-                send = fwd_send.at[6 * (q % 4) + e if q < 8 else 24 + 2 * (q - 8) + e]
+                send = fwd_send.at[(6 * q if q < 4 else 24 + 4 * (q - 4) if q < 8 else 40 + 2 * (q - 8)) + e]
                 yield on, remote(src, dst, send, fwd_recv.at[q, 0 if db > 0 else 1], target)
 
     def wait_sent(*slots):
@@ -331,25 +332,25 @@
                       hop_send.at[db + 3], hop_recv.at[3 - db], target)
 
     def source_images(q, row):
-        dd, f = ew - SLOTS + q, p % 2
+        dd, f = ew - SLOTS + q, (p & 1)
         for half in range(2):
             yield half, remote(x_all.at[:, pl.ds(pl.multiple_of(row + HALF * half, 8), HALF), :], out_s.at[f],
-                               im_send.at[q % 4, half], ims_recv.at[f], (dd, 2 * b + half))
+                               im_send.at[q, half], ims_recv.at[f], (dd, 2 * b + half))
 
     def receiver_images(q, row):
-        dd, f = ew - SLOTS + q, p % 2
+        dd, f = ew - SLOTS + q, (p & 1)
         for half in range(2):
             yield half, remote(x_all.at[:, pl.ds(pl.multiple_of(row + 8 * half, 8), 24), :],
                                out_r.at[f, :, pl.ds(8 - 8 * half, 24), :],
-                               im_send.at[q % 4, half], imr_recv.at[f, 0], (dd, 2 * b + half))
+                               im_send.at[q, half], imr_recv.at[f, 0], (dd, 2 * b + half))
 
     def edge_images(q, row):
-        dd, f = ew - SLOTS + q, p % 2
+        dd, f = ew - SLOTS + q, (p & 1)
         for half in range(2):
             on = b > 0 if half == 0 else b < BLOCKS - 1
             yield on, remote(x_all.at[:, pl.ds(pl.multiple_of(row + 24 * half, 8), 8), :],
                              out_r.at[f, :, pl.ds(24 - 24 * half, 8), :],
-                             im_send.at[q % 4, 2 + half], imr_recv.at[f, 1], (dd, 2 * b - 1 + 3 * half))
+                             im_send.at[q, 2 + half], imr_recv.at[f, 1], (dd, 2 * b - 1 + 3 * half))
 
     def send_images(q, level):
         base, own = x_row(level) if not isinstance(level, int) else (X_BASE[level], REACH * (LEVELS - level))
@@ -370,14 +371,14 @@
 
         def local_source(half):
             copy = pltpu.make_async_copy(
-                x_all.at[:, pl.ds(pl.multiple_of(row + HALF * half, 8), HALF), :], out_s.at[p % 2], self_sem.at[2])
+                x_all.at[:, pl.ds(pl.multiple_of(row + HALF * half, 8), HALF), :], out_s.at[(p & 1)], self_sem.at[2])
             copy.start()
             copy.wait()
 
         def local_receiver(half):
             copy = pltpu.make_async_copy(
                 x_all.at[:, pl.ds(pl.multiple_of(row + 8 * half, 8), 24), :],
-                out_r.at[p % 2, :, pl.ds(8 - 8 * half, 24), :], self_sem.at[2])
+                out_r.at[(p & 1), :, pl.ds(8 - 8 * half, 24), :], self_sem.at[2])
             copy.start()
             copy.wait()
 
@@ -478,7 +479,7 @@
 
     @pl.when(is_w)
     def _():
-        f = p % 2
+        f = (p & 1)
         tab_copy.wait()
         for t in range(2 * len(TAPS)):
             tab8[t] = jnp.broadcast_to(tab_ref[t // 2, t % 2, pl.ds(f, 1), :], (8, 128))
@@ -496,48 +497,23 @@
                 lax.fori_loop(q0, SLOTS, clear, 0)
                 row = own + ROWS * db
 
-                @pl.when(both(row >= 0, ROWS * db < ROWS + own))
+                @pl.when(sw >= (0, 1, 3)[abs(db) - 1])
                 def _():
                     x_all[:, pl.ds(pl.multiple_of(base + row, 8), ROWS), :] = zf
 
     @pl.when(is_w)
     def _():
-        @pl.when(sw >= 1)
-        def _():
-            forward(4)
-
-        forward(8)
-
-        @pl.when(sw >= 1)
-        def _():
-            forward(5)
-
-        forward(9)
-        wait_forwarded(8)
-        look_up_slots(8, 9)
-
-        @pl.when(sw >= 1)
-        def _():
-            wait_forwarded(4)
-            look_up_slots(4, 5)
-            forward(6)
-
-        forward(10)
-        wait_forwarded(9)
-
-        @pl.when(sw >= 1)
-        def _():
-            wait_forwarded(5)
-            look_up_slots(5, 6)
-            forward(7)
-
-            @pl.when(sw == 3)
-            def _():
-                wait_sent(4, 5, 6, 7)
-                forward(0, 1, 2, 3)
+        def look_up_last():
+            wait_own(SLOTS - 1)
+            wait_forwarded(SLOTS - 1)
+            look_up(SLOTS - 1, 4)
 
         @pl.when(sw == 0)
         def _():
+            forward(8, 9)
+            wait_forwarded(8)
+            look_up(8, GATHER)
+
             for g in range(6):
                 jj = 2 * b - 2 + g
 
@@ -555,29 +531,58 @@
 
             apply(16)
             apply(17)
-
-        look_up_slots(9, 10)
-        wait_forwarded(10)
-        look_up_slots(10, 11)
-
-        @pl.when(sw == 0)
-        def _():
-            for i in range(18, 22):
-                apply(i)
+            forward(10)
+            wait_forwarded(9)
+            look_up(9, GATHER)
+            apply(18)
+            apply(19)
+            wait_forwarded(10)
+            look_up(10, GATHER)
+            apply(20)
+            apply(21)
+            look_up_last()
 
         @pl.when(sw >= 1)
         def _():
-            wait_forwarded(6, 7)
-            look_up_slots(6, 8)
-
-        wait_own(SLOTS - 1)
-        wait_forwarded(SLOTS - 1)
-        look_up(SLOTS - 1, 4)
-
-        @pl.when(sw == 3)
-        def _():
-            wait_forwarded(0, 1, 2, 3)
-            look_up_slots(0, 4)
+            forward(4, 8, 5, 9)
+
+            @pl.when(sw == 3)
+            def _():
+                forward(0, 1)
+
+            wait_forwarded(4)
+            look_up(4, 9)
+            wait_forwarded(8)
+            look_up(8, GATHER)
+            forward(6, 10)
+
+            @pl.when(sw == 3)
+            def _():
+                forward(2)
+
+            wait_forwarded(5)
+            look_up(5, 9)
+            forward(7)
+
+            @pl.when(sw == 3)
+            def _():
+                forward(3)
+
+            wait_forwarded(6)
+            look_up(6, 9)
+            wait_forwarded(9, 10)
+            look_up_slots(9, 11)
+            wait_forwarded(7)
+            look_up(7, GATHER)
+            look_up_last()
+
+            @pl.when(sw == 3)
+            def _():
+                wait_forwarded(0, 1, 2, 3)
+                look_up(3, 12)
+                look_up(2, 12)
+                look_up(1, 9)
+                look_up(0, 9)
 
         @pl.when(is_later)
         def _():
@@ -595,20 +600,16 @@
 
             @pl.when(sw == 3)
             def _():
-                if q >= 4:
-                    wait_images(q - 4)
                 send_images(q, 2 * q + 2)
 
-        @pl.when(sw == 3)
-        def _():
-            for q in range(4):
-                slab(q)
-
-        @pl.when(sw >= 1)
-        def _():
-            for q in range(4, SLOTS - 1):
-                slab(q)
-
+        def slabs(on, start, end):
+            @pl.when(on)
+            def _():
+                for q in range(start, end):
+                    slab(q)
+
+        slabs(sw == 3, 0, 4)
+        slabs(sw >= 1, 4, SLOTS - 1)
         slab(SLOTS - 1)
 
         @pl.when(is_earlier)
@@ -624,10 +625,6 @@
                     hop_copy(db, target).start()
 
             def slot(q, c):
-                @pl.when(q - 4 >= q0)
-                def _():
-                    wait_images(q - 4)
-
                 send_images(q, 2 * q + 2)
                 return c
 
@@ -673,7 +670,7 @@
         def _():
             wait_sent(0, 1, 2, 3)
 
-        @pl.when(both(sw >= 1, sw <= 2))
+        @pl.when(sw >= 1)
         def _():
             wait_sent(4, 5, 6, 7)
 
@@ -691,7 +688,7 @@
             wait_images(q)
             return c
 
-        lax.fori_loop(SLOTS - 4, SLOTS, slot, 0)
+        lax.fori_loop(q0, SLOTS, slot, 0)
 
 
 def image_kernel(offsets, s_ref, r_ref, out_ref):
@@ -727,9 +724,9 @@
             pltpu.VMEM(stencil_table.shape, f32),
             pltpu.VMEM((2, 2, OFF_Y, 128), f32),
             dma, dma((3,)), dma,
-            dma((4,)), dma((SLOTS,)), dma((4,)), dma((30,)), dma((SLOTS, 2)),
+            dma((4,)), dma((SLOTS,)), dma((4,)), dma((46,)), dma((SLOTS, 2)),
             dma((3,)), dma((6,)), dma((7,)), dma((7,)),
-            dma((4, 4)), dma((2,)), dma((2, 2)), pltpu.SemaphoreType.REGULAR,
+            dma((SLOTS, 4)), dma((2,)), dma((2, 2)), pltpu.SemaphoreType.REGULAR,
         ],
         compiler_params=pltpu.CompilerParams(
             collective_id=0, has_side_effects=True, vmem_limit_bytes=56 * 2**20),

time: 63.2 us -> 59.1 us (0.935)
  Pallas kernels: 63 us -> 58.9 us
    pallas_call x1, Pallas kernels: 61.3 us -> 57.2 us  [shards(): pl.pallas_call(chain_kernel, out_shape=(jax.ShapeDtypeStruct((2, 2, 16, 1...]
where the time goes in v3:
time: 59.1 us; the launch traced here: 58.9 us
  Pallas kernels  58.9 us (100%)
    pallas_call x1, Pallas kernels, shards(): pl.pallas_call(chain_kernel, out_shape=(jax.ShapeDtypeStruct((2, 2, 16, 1...  57.2 us
    pallas_call x1, Pallas kernels, shards(): pl.pallas_call(image_kernel, out_shape=jax.ShapeDtypeStruct((1, offset_li...  1.74 us

profile of v3, /device:TPU:58, one launch (start us, length us, event | category | flops | bytes accessed | tf_op | source)
XLA Modules:
  0.0 58.9 jit_solution(8386426358803005105)
XLA Ops:
  0.0 57.2 %shard_map.46 = (f32[2,2,16,128]{3,2,1,0:T(8,128)}, f32[2,2,32,128]{3,2,1,0:T(8,128)}) custom-call(f32[2,2,2,16,128]{4,3,2,1,0:T(8,128)} %surf_ref.1, f32[13,2,2,128]{3,2,1,0:T(2,128)} %tab_hbm.1, s32[1,2,16,128]{3,2,1,0:T(8,128)} %bins_ref.1), custom_call_target="tpu_custom_call" | custom-call | tf_op jit(solution)/shard_map/pallas_call | solution.py:714
  57.2 1.7 %shard_map.47 = f32[1,16,16,128]{3,2,1,0:T(8,128)} custom-call(s32[2,16]{1,0:T(2,128)} %bitcast.1, f32[2,2,16,128]{3,2,1,0:T(8,128)} %get-tuple-element.7.s_ref, f32[2,2,32,128]{3,2,1,0:T(8,128)} %get-tuple-element.8.r_ref), custom_call_target="tpu_custom_call" | custom-call | tf_op jit(solution)/shard_map/pallas_call | solution.py:734
